TPU v7x, 512 devices: a whole 4x4x16 slice. The times are simulated.
512 devices in a mesh: sec: 16 (over z), gx: 16 (over y_lo, x, core), gy: 2 (over y_hi).
Axes of the slice: x: 4, y: 4 (y_hi: 2, y_lo: 2; y = y_hi * 2 + y_lo), z: 16, core: 2. Of those that a mesh axis runs over, the one named last changes fastest.
Arguments:
- number: float32 [128, 4, 128, 256], P('sec', None, 'gx', 'gy'), may hold values from 0.05 to 1
- cotangent: float32 [128, 4, 128, 256], P('sec', None, 'gx', 'gy'), may hold values from -6 to 6
- growth_rate: float32 [4, 128, 256], P(None, 'gx', 'gy'), may hold values from 1 to 10000
- section_factor: float32 [128], replicated, may hold values from 0.5 to 2
- velocity: float32 [2, 4, 128, 256], P(None, None, 'gx', 'gy'), may hold values from -1 to 1
- diffusivity: float32 [128], replicated, may hold values from 0.05 to 0.4
- kernel: float32 [128, 128], replicated, may hold values from 0.001 to 0.03
- target: int32 [128, 128], replicated, may hold values from 0 to 127, as said below
Outputs:
- number_next: float32 [128, 4, 128, 256], P('sec', None, 'gx', 'gy')
- gradient: float32 [128, 4, 128, 256], P('sec', None, 'gx', 'gy')
Inputs may be any that keep to these rules, and one draw needn't show every extreme that they name: target[i, j] is at least the larger of i and j.
All inputs are finite; a program needn't handle non-finite values.
Results may differ from a plain program's by a relative error of at most 0.0001.
Values sent between devices are 32-bit elements; how exact they have to be, the bound alone decides.
No kernel may reach another device: no remote copies, remote signals or barrier semaphores. Data moves between devices by JAX's collectives and lax.ppermute only.
A program may use at most 64 MiB of HBM per device.

v0:
```python
import jax
import jax.numpy as jnp
from jax import lax
from jax.sharding import PartitionSpec as P

step_size = 0.25
vertical_mix = 0.2
highest = lax.Precision.HIGHEST


def padded_2(block, sides, width):
    for axis, dim in sides:
        count = lax.axis_size(axis)
        forward = [(i, i + 1) for i in range(count - 1)]
        forward.append((count - 1, 0))
        backward = [(target, source) for source, target in forward]
        low = lax.ppermute(
            lax.slice_in_dim(block, block.shape[dim] - width, None, axis=dim), axis, forward
        )
        high = lax.ppermute(lax.slice_in_dim(block, 0, width, axis=dim), axis, backward)
        block = jnp.concatenate([low, block, high], axis=dim)
    return block


def vertical(field):
    widths = [(0, 0)] * (field.ndim - 3) + [(1, 1), (0, 0), (0, 0)]
    extended = jnp.pad(field, widths, mode="edge")
    return extended[..., 2:, :, :] + extended[..., :-2, :, :] - 2.0 * field


def stencil(padded):
    center = padded[..., 1:-1, 1:-1]
    return (
        center,
        padded[..., 2:, 1:-1],
        padded[..., :-2, 1:-1],
        padded[..., 1:-1, 2:],
        padded[..., 1:-1, :-2],
    )


def forward_transport(padded, velocity, diffusion):
    center, x_plus, x_minus, y_plus, y_minus = stencil(padded)
    return (
        -velocity[0] * (x_plus - x_minus) * 0.5
        - velocity[1] * (y_plus - y_minus) * 0.5
        + diffusion * (x_plus + x_minus + y_plus + y_minus - 4.0 * center)
        + vertical_mix * vertical(center)
    )


def adjoint_transport(padded_adj, padded_fx, padded_fy, diffusion):
    center, x_plus, x_minus, y_plus, y_minus = stencil(padded_adj)
    flux_x = padded_fx[..., 2:, 1:-1] - padded_fx[..., :-2, 1:-1]
    flux_y = padded_fy[..., 1:-1, 2:] - padded_fy[..., 1:-1, :-2]
    return (
        flux_x * 0.5
        + flux_y * 0.5
        + diffusion * (x_plus + x_minus + y_plus + y_minus - 4.0 * center)
        + vertical_mix * vertical(center)
    )


def compose(earlier, later):
    return (later[0] * earlier[0], later[0] * earlier[1] + later[1])


def pair_terms(all_number, all_adjoint, kernel, target, first_row, row_count, group_size):
    sections, cell_count = all_number.shape
    section_ids = lax.broadcasted_iota(jnp.int32, (1, sections, 1), 1)

    def visit(turn, carried):
        gain_sum, spread, own_rows = carried
        start = first_row + turn * group_size
        half_rows = 0.5 * lax.dynamic_slice_in_dim(kernel, start, group_size, 0)
        target_rows = lax.dynamic_slice_in_dim(target, start, group_size, 0)
        weights = jnp.where(target_rows[:, None, :] == section_ids, half_rows[:, None, :], 0.0)
        number_block = lax.dynamic_slice_in_dim(all_number, start, group_size, 0)
        products = jnp.einsum("atj,jc->atc", weights, all_number, precision=highest)
        gain_sum = gain_sum + jnp.sum(products * number_block[:, None, :], axis=0)
        lookup = jnp.einsum("atj,tc->ajc", weights, all_adjoint, precision=highest)
        own_block = jnp.sum(lookup * all_number[None], axis=1)
        own_rows = lax.dynamic_update_slice_in_dim(own_rows, own_block, turn * group_size, 0)
        spread = spread + jnp.sum(lookup * number_block[:, None, :], axis=0)
        return (gain_sum, spread, own_rows)

    zero_field = jnp.zeros((sections, cell_count), jnp.float32)
    start_state = (zero_field, zero_field, jnp.zeros((row_count, cell_count), jnp.float32))
    gain_sum, spread, own_rows = lax.fori_loop(0, row_count // group_size, visit, start_state)
    pull = jnp.dot(kernel, all_number, precision=highest)
    loss_rows = all_number * pull
    back_pull = jnp.einsum("sk,sc->kc", kernel, all_adjoint * all_number, precision=highest)
    loss_adjoint = -all_adjoint * pull - back_pull
    return (gain_sum, spread, own_rows, loss_rows, loss_adjoint)


def per_device(
    number, cotangent, growth_rate, section_factor, velocity, diffusivity, kernel, target
):
    sections = kernel.shape[0]
    block_rows = number.shape[0]
    cell_count = number.shape[1] * number.shape[2] * number.shape[3]
    device_index = lax.axis_index("sec")
    first_row = device_index * block_rows
    diffusion = lax.dynamic_slice_in_dim(diffusivity, first_row, block_rows)[:, None, None, None]
    prior_all = jnp.concatenate([jnp.zeros((1,), jnp.float32), section_factor[:-1]])
    rate_cells = growth_rate.reshape(cell_count)
    flat_number = number.reshape(block_rows, cell_count)
    flat_cot = cotangent.reshape(block_rows, cell_count)
    padded_state = padded_2(number, (("gx", 2), ("gy", 3)), 1)
    advected = forward_transport(padded_state, velocity, diffusion).reshape(block_rows, cell_count)
    piece_cells = cell_count // lax.axis_size("sec")
    cell_number, cell_advected, cell_cot = (
        lax.all_to_all(flat_number, "sec", split_axis=1, concat_axis=0, tiled=True),
        lax.all_to_all(advected, "sec", split_axis=1, concat_axis=0, tiled=True),
        lax.all_to_all(flat_cot, "sec", split_axis=1, concat_axis=0, tiled=True),
    )
    rate_piece = lax.dynamic_slice_in_dim(rate_cells, device_index * piece_cells, piece_cells)
    step_rate = step_size * (section_factor[:, None] * rate_piece[None, :])
    prior_rate = step_size * (prior_all[:, None] * rate_piece[None, :])
    span_c, cell_adjoint = lax.associative_scan(
        compose, (step_rate / (1.0 + step_rate), cell_cot / (1.0 + step_rate)), axis=0, reverse=True
    )
    gain_sum, spread, own_rows, loss_rows, loss_adjoint = pair_terms(
        cell_number, cell_adjoint, kernel, target, 0, sections, 8
    )
    explicit = cell_number + step_size * (cell_advected + gain_sum - loss_rows)
    span_a, cell_next = lax.associative_scan(
        compose, (prior_rate / (1.0 + step_rate), explicit / (1.0 + step_rate)), axis=0
    )
    cell_coag = own_rows + spread + loss_adjoint
    number_next, coag_terms, adjoint = (
        lax.all_to_all(cell_next, "sec", split_axis=0, concat_axis=1, tiled=True),
        lax.all_to_all(cell_coag, "sec", split_axis=0, concat_axis=1, tiled=True),
        lax.all_to_all(cell_adjoint, "sec", split_axis=0, concat_axis=1, tiled=True),
    )
    adjoint_grid = adjoint.reshape(number.shape)
    stacked = jnp.stack([adjoint_grid, velocity[0] * adjoint_grid, velocity[1] * adjoint_grid])
    padded = padded_2(stacked, (("gx", 3), ("gy", 4)), 1)
    transported = adjoint_transport(padded[0], padded[1], padded[2], diffusion).reshape(
        block_rows, cell_count
    )
    gradient = adjoint + step_size * (transported + coag_terms)
    return (number_next.reshape(number.shape), gradient.reshape(number.shape))


def solution(mesh):
    return jax.shard_map(
        per_device,
        mesh=mesh,
        in_specs=(
            P("sec", None, "gx", "gy"),
            P("sec", None, "gx", "gy"),
            P(None, "gx", "gy"),
            P(),
            P(None, None, "gx", "gy"),
            P(),
            P(),
            P(),
        ),
        out_specs=(P("sec", None, "gx", "gy"), P("sec", None, "gx", "gy")),
        check_vma=False,
    )
```

profile of v0, /device:TPU:1, one launch (start us, length us, event | category | flops | bytes accessed | tf_op | source)
XLA Modules:
  0.0 220.8 jit_solution(13135573858110365280)
XLA Ops:
  0.7 1.0 all_to_all.90
  1.6 0.7 copy.64
  2.4 15.7 %all-to-all-start.2 = ((f32[8,16,256]{2,0,1:T(8,128)}), f32[8,16,256]{2,0,1:T(8,128)S(1)}, u32[]{:S(2)}, u32[]{:S(2)}) async-start(f32[8,16,256]{2,0,1:T(8,128)} %copy.64), calls=%async_computation.2 | async-start | bytes 262144 | tf_op jit(solution)/shard_map/all_to_all | solution.py:116
  18.1 1.0 fusion.61
  19.1 2.9 %collective-permute-start = (f32[8,4,1,128]{3,2,1,0:T(1,128)S(1)}, f32[8,4,1,128]{3,2,1,0:T(1,128)S(1)}, u32[]{:S(2)}, u32[]{:S(2)}) collective-permute-start(f32[8,4,1,128]{3,2,1,0:T(1,128)S(1)} %get-tuple-element.226), channel_id=1, source_target_pairs={{2,0},{4,2},{6,4},{8,6},{10,8},{12,10},{14,12},{16,14},{18,16},{20... | collective-permute-start | bytes 49160 | tf_op jit(solution)/shard_map/ppermute | solution.py:20
  22.0 3.0 %collective-permute-start.1 = (f32[8,4,1,128]{3,2,1,0:T(1,128)S(1)}, f32[8,4,1,128]{3,2,1,0:T(1,128)S(1)}, u32[]{:S(2)}, u32[]{:S(2)}) collective-permute-start(f32[8,4,1,128]{3,2,1,0:T(1,128)S(1)} %get-tuple-element.225), channel_id=1, source_target_pairs={{0,2},{2,4},{4,6},{6,8},{8,10},{10,12},{12,14},{14,16},{16,18},{18... | collective-permute-start | bytes 49160 | tf_op jit(solution)/shard_map/ppermute | solution.py:17
  25.0 0.8 fusion.62
  25.8 0.7 slice_bitcast_fusion.4
  27.3 0.9 all_to_all.82
  28.3 1.0 pad_maximum_fusion.2
  29.4 4.8 %collective-permute-start.2 = (f32[8,4,10,1]{3,2,1,0:T(8,128)S(1)}, f32[8,4,10,1]{3,2,1,0:T(8,128)S(1)}, u32[]{:S(2)}, u32[]{:S(2)}) collective-permute-start(f32[8,4,10,1]{3,2,1,0:T(8,128)S(1)} %get-tuple-element.222), channel_id=1, source_target_pairs={{1,0},{0,1},{3,2},{2,3},{5,4},{4,5},{7,6},{6,7},{9,8},{8,9},{11,10... | collective-permute-start | bytes 3848 | tf_op jit(solution)/shard_map/ppermute | solution.py:20
  34.2 2.0 collective-permute-start.3
  36.9 0.8 dynamic_slice.28
  38.0 7.9 %collective-permute-done.3 = f32[8,4,10,1]{3,2,1,0:T(8,128)S(1)} collective-permute-done((f32[8,4,10,1]{3,2,1,0:T(8,128)S(1)}, f32[8,4,10,1]{3,2,1,0:T(8,128)S(1)}, u32[]{:S(2)}, u32[]{:S(2)}) %collective-permute-start.3) | collective-permute-done | bytes 1312 | tf_op jit(solution)/shard_map/ppermute | solution.py:17
  46.9 11.8 %all-to-all-start = ((f32[8,16,256]{2,0,1:T(8,128)}), f32[8,16,256]{2,0,1:T(8,128)S(1)}, u32[]{:S(2)}, u32[]{:S(2)}) async-start(f32[8,16,256]{2,0,1:T(8,128)} %copy.62), calls=%async_computation | async-start | bytes 262144 | tf_op jit(solution)/shard_map/all_to_all | solution.py:114
  61.5 9.2 %all-to-all-done = f32[8,16,256]{2,0,1:T(8,128)S(1)} async-done(((f32[8,16,256]{2,0,1:T(8,128)}), f32[8,16,256]{2,0,1:T(8,128)S(1)}, u32[]{:S(2)}, u32[]{:S(2)}) %all-to-all-start) | async-done | bytes 131104 | tf_op jit(solution)/shard_map/all_to_all | solution.py:114
  70.7 4.0 %all-to-all-start.1 = ((f32[8,16,256]{2,0,1:T(8,128)}), f32[8,16,256]{2,0,1:T(8,128)S(1)}, u32[]{:S(2)}, u32[]{:S(2)}) async-start(f32[8,16,256]{2,0,1:T(8,128)} %copy.63), calls=%async_computation.1 | async-start | bytes 262144 | tf_op jit(solution)/shard_map/all_to_all | solution.py:115
  74.8 67.2 %while.18 = (s32[]{:T(128)}, f32[128,256]{1,0:T(8,128)S(1)}, f32[128,256]{1,0:T(8,128)S(1)}, f32[128,256]{1,0:T(8,128)S(1)}, s32[128,128]{1,0:T(8,128)}, /*index...) while((s32[]{:T(128)}, f32[128,256]{1,0:T(8,128)S(1)}, ...), condition=%wide.region_4.5_spmd.clone, body=%wide.region_0.4_spmd.clone.sunk | while | flops 807468032 | bytes 1532093 | solution.py:89
  75.5 2.0 multiply_reduce_fusion.3
  77.4 1.4 fusion.82
  79.7 2.0 multiply_reduce_fusion.3
  81.7 1.4 fusion.82
  83.9 2.0 multiply_reduce_fusion.3
  85.9 1.4 fusion.82
  88.1 2.0 multiply_reduce_fusion.3
  90.1 1.4 fusion.82
  92.3 2.0 multiply_reduce_fusion.3
  94.3 1.4 fusion.82
  96.5 2.0 multiply_reduce_fusion.3
  98.5 1.4 fusion.82
  100.7 2.0 multiply_reduce_fusion.3
  102.7 1.4 fusion.82
  104.9 2.0 multiply_reduce_fusion.3
  106.9 1.4 fusion.82
  109.1 2.0 multiply_reduce_fusion.3
  111.1 1.4 fusion.82
  113.3 2.0 multiply_reduce_fusion.3
  115.3 1.4 fusion.82
  117.5 2.0 multiply_reduce_fusion.3
  119.5 1.4 fusion.82
  121.7 2.0 multiply_reduce_fusion.3
  123.7 1.4 fusion.82
  125.9 2.0 multiply_reduce_fusion.3
  127.9 1.4 fusion.82
  130.1 2.0 multiply_reduce_fusion.3
  132.1 1.4 fusion.82
  134.3 2.0 multiply_reduce_fusion.3
  136.3 1.4 fusion.82
  138.5 2.0 multiply_reduce_fusion.3
  140.5 1.4 fusion.82
  142.3 1.9 fusion.18
  144.2 11.5 %all-to-all-start.4 = ((f32[16,8,256]{2,1,0:T(8,128)}), f32[16,8,256]{2,1,0:T(8,128)S(1)}, u32[]{:S(2)}, u32[]{:S(2)}) async-start(f32[16,8,256]{2,1,0:T(8,128)} %bitcast.12), calls=%async_computation.4 | async-start | bytes 262144 | tf_op jit(solution)/shard_map/all_to_all | solution.py:135
  157.1 10.6 %all-to-all-done.4 = f32[16,8,256]{2,1,0:T(8,128)S(1)} async-done(((f32[16,8,256]{2,1,0:T(8,128)}), f32[16,8,256]{2,1,0:T(8,128)S(1)}, u32[]{:S(2)}, u32[]{:S(2)}) %all-to-all-start.4) | async-done | bytes 131104 | tf_op jit(solution)/shard_map/all_to_all | solution.py:135
  167.7 4.0 %all-to-all-start.5 = ((f32[16,8,256]{2,1,0:T(8,128)}), f32[16,8,256]{2,1,0:T(8,128)S(1)}, u32[]{:S(2)}, u32[]{:S(2)}) async-start(f32[16,8,256]{2,1,0:T(8,128)} %fusion.18), calls=%async_computation.5 | async-start | bytes 262144 | tf_op jit(solution)/shard_map/all_to_all | solution.py:134
  172.6 11.1 %all-to-all-done.5 = f32[16,8,256]{2,1,0:T(8,128)S(1)} async-done(((f32[16,8,256]{2,1,0:T(8,128)}), f32[16,8,256]{2,1,0:T(8,128)S(1)}, u32[]{:S(2)}, u32[]{:S(2)}) %all-to-all-start.5) | async-done | bytes 131104 | tf_op jit(solution)/shard_map/all_to_all | solution.py:134
  183.7 4.0 %all-to-all-start.3 = ((f32[16,8,256]{2,1,0:T(8,128)}), f32[16,8,256]{2,1,0:T(8,128)S(1)}, u32[]{:S(2)}, u32[]{:S(2)}) async-start(f32[16,8,256]{2,1,0:T(8,128)} %add_bitcast_fusion), calls=%async_computation.3 | async-start | bytes 262144 | tf_op jit(solution)/shard_map/all_to_all | solution.py:133
  187.8 11.2 %collective-permute-start.4 = (f32[3,8,4,1,128]{4,3,2,1,0:T(1,128)S(1)}, f32[3,8,4,1,128]{4,3,2,1,0:T(1,128)S(1)}, u32[]{:S(2)}, u32[]{:S(2)}) collective-permute-start(f32[3,8,4,1,128]{4,3,2,1,0:T(1,128)S(1)} %get-tuple-element.219), channel_id=1, source_target_pairs={{0,2},{2,4},{4,6},{6,8},{8,10},{10,12},{12,14},{14,16},{16,18},{18... | collective-permute-start | bytes 147464 | tf_op jit(solution)/shard_map/ppermute | solution.py:17
  199.0 1.9 collective-permute-start.5
  201.0 3.8 %collective-permute-done.5 = f32[3,8,4,1,128]{4,3,2,1,0:T(1,128)S(1)} collective-permute-done((f32[3,8,4,1,128]{4,3,2,1,0:T(1,128)S(1)}, f32[3,8,4,1,128]{4,3,2,1,0:T(1,128)S(1)}, u32[]{:S(2)}, u32[]{:S(2)}) %collective-permute-start.5) | collective-permute-done | bytes 49184 | tf_op jit(solution)/shard_map/ppermute | solution.py:20
  205.8 4.8 %collective-permute-start.6 = (f32[3,8,4,10,1]{3,1,4,2,0:T(8,128)S(1)}, f32[3,8,4,10,1]{3,1,4,2,0:T(8,128)S(1)}, u32[]{:S(2)}, u32[]{:S(2)}) collective-permute-start(f32[3,8,4,10,1]{3,1,4,2,0:T(8,128)S(1)} %copy.68), channel_id=1, source_target_pairs={{0,1},{1,0},{2,3},{3,2},{4,5},{5,4},{6,7},{7,6},{8,9},{9,8},{10,11... | collective-permute-start | bytes 11528 | tf_op jit(solution)/shard_map/ppermute | solution.py:17
  211.3 2.0 collective-permute-start.7
  214.8 2.9 %collective-permute-done.7 = f32[3,8,4,10,1]{3,1,4,2,0:T(8,128)S(1)} collective-permute-done((f32[3,8,4,10,1]{3,1,4,2,0:T(8,128)S(1)}, f32[3,8,4,10,1]{3,1,4,2,0:T(8,128)S(1)}, u32[]{:S(2)}, u32[]{:S(2)}) %collective-permute-start.7) | collective-permute-done | bytes 3872 | tf_op jit(solution)/shard_map/ppermute | solution.py:20
  218.4 1.1 pad_maximum_fusion
  219.8 1.0 fusion.25
  (288 shorter events, 24.5 us)
Async XLA Ops:
  0.6 45.2 %copy-start = (f32[8,4,8,128]{3,2,1,0:T(8,128)S(1)}, f32[8,4,8,128]{3,2,1,0:T(8,128)}, u32[]{:S(2)}) copy-start(f32[8,4,8,128]{3,2,1,0:T(8,128)} %param.10) | copy-start | bytes 393220
  0.6 37.0 %copy-start.3 = (f32[128]{0:T(128)S(1)}, f32[128]{0:T(128)}, u32[]{:S(2)}) copy-start(f32[128]{0:T(128)} %param.15) | copy-start | bytes 1540
  2.4 44.5 %all-to-all-start.2 = ((f32[8,16,256]{2,0,1:T(8,128)}), f32[8,16,256]{2,0,1:T(8,128)S(1)}, u32[]{:S(2)}, u32[]{:S(2)}) async-start(f32[8,16,256]{2,0,1:T(8,128)} %copy.64), calls=%async_computation.2 | async-start | bytes 262144 | tf_op jit(solution)/shard_map/all_to_all | solution.py:116
  19.1 9.1 %collective-permute-start = (f32[8,4,1,128]{3,2,1,0:T(1,128)S(1)}, f32[8,4,1,128]{3,2,1,0:T(1,128)S(1)}, u32[]{:S(2)}, u32[]{:S(2)}) collective-permute-start(f32[8,4,1,128]{3,2,1,0:T(1,128)S(1)} %get-tuple-element.226), channel_id=1, source_target_pairs={{2,0},{4,2},{6,4},{8,6},{10,8},{12,10},{14,12},{16,14},{18,16},{20... | collective-permute-start | bytes 49160 | tf_op jit(solution)/shard_map/ppermute | solution.py:20
  22.0 6.3 %collective-permute-start.1 = (f32[8,4,1,128]{3,2,1,0:T(1,128)S(1)}, f32[8,4,1,128]{3,2,1,0:T(1,128)S(1)}, u32[]{:S(2)}, u32[]{:S(2)}) collective-permute-start(f32[8,4,1,128]{3,2,1,0:T(1,128)S(1)} %get-tuple-element.225), channel_id=1, source_target_pairs={{0,2},{2,4},{4,6},{6,8},{8,10},{10,12},{12,14},{14,16},{16,18},{18... | collective-permute-start | bytes 49160 | tf_op jit(solution)/shard_map/ppermute | solution.py:17
  29.2 29.5 %copy-start.2 = (f32[128]{0:T(128)S(1)}, f32[128]{0:T(128)}, u32[]{:S(2)}) copy-start(f32[128]{0:T(128)} %param.13) | copy-start | bytes 1540
  29.4 8.6 %collective-permute-start.2 = (f32[8,4,10,1]{3,2,1,0:T(8,128)S(1)}, f32[8,4,10,1]{3,2,1,0:T(8,128)S(1)}, u32[]{:S(2)}, u32[]{:S(2)}) collective-permute-start(f32[8,4,10,1]{3,2,1,0:T(8,128)S(1)} %get-tuple-element.222), channel_id=1, source_target_pairs={{1,0},{0,1},{3,2},{2,3},{5,4},{4,5},{7,6},{6,7},{9,8},{8,9},{11,10... | collective-permute-start | bytes 3848 | tf_op jit(solution)/shard_map/ppermute | solution.py:20
  34.2 11.7 %collective-permute-start.3 = (f32[8,4,10,1]{3,2,1,0:T(8,128)S(1)}, f32[8,4,10,1]{3,2,1,0:T(8,128)S(1)}, u32[]{:S(2)}, u32[]{:S(2)}) collective-permute-start(f32[8,4,10,1]{3,2,1,0:T(8,128)S(1)} %get-tuple-element.221), channel_id=1, source_target_pairs={{0,1},{1,0},{2,3},{3,2},{4,5},{5,4},{6,7},{7,6},{8,9},{9,8},{10,11... | collective-permute-start | bytes 3848 | tf_op jit(solution)/shard_map/ppermute | solution.py:17
  46.9 23.8 %all-to-all-start = ((f32[8,16,256]{2,0,1:T(8,128)}), f32[8,16,256]{2,0,1:T(8,128)S(1)}, u32[]{:S(2)}, u32[]{:S(2)}) async-start(f32[8,16,256]{2,0,1:T(8,128)} %copy.62), calls=%async_computation | async-start | bytes 262144 | tf_op jit(solution)/shard_map/all_to_all | solution.py:114
  60.2 14.5 %copy-start.1 = (f32[128,128]{1,0:T(8,128)S(1)}, f32[128,128]{1,0:T(8,128)}, u32[]{:S(2)}) copy-start(f32[128,128]{1,0:T(8,128)} %param.16) | copy-start | bytes 196612
  70.7 73.5 %all-to-all-start.1 = ((f32[8,16,256]{2,0,1:T(8,128)}), f32[8,16,256]{2,0,1:T(8,128)S(1)}, u32[]{:S(2)}, u32[]{:S(2)}) async-start(f32[8,16,256]{2,0,1:T(8,128)} %copy.63), calls=%async_computation.1 | async-start | bytes 262144 | tf_op jit(solution)/shard_map/all_to_all | solution.py:115
  144.2 23.4 %all-to-all-start.4 = ((f32[16,8,256]{2,1,0:T(8,128)}), f32[16,8,256]{2,1,0:T(8,128)S(1)}, u32[]{:S(2)}, u32[]{:S(2)}) async-start(f32[16,8,256]{2,1,0:T(8,128)} %bitcast.12), calls=%async_computation.4 | async-start | bytes 262144 | tf_op jit(solution)/shard_map/all_to_all | solution.py:135
  167.7 16.0 %all-to-all-start.5 = ((f32[16,8,256]{2,1,0:T(8,128)}), f32[16,8,256]{2,1,0:T(8,128)S(1)}, u32[]{:S(2)}, u32[]{:S(2)}) async-start(f32[16,8,256]{2,1,0:T(8,128)} %fusion.18), calls=%async_computation.5 | async-start | bytes 262144 | tf_op jit(solution)/shard_map/all_to_all | solution.py:134
  183.7 29.7 %all-to-all-start.3 = ((f32[16,8,256]{2,1,0:T(8,128)}), f32[16,8,256]{2,1,0:T(8,128)S(1)}, u32[]{:S(2)}, u32[]{:S(2)}) async-start(f32[16,8,256]{2,1,0:T(8,128)} %add_bitcast_fusion), calls=%async_computation.3 | async-start | bytes 262144 | tf_op jit(solution)/shard_map/all_to_all | solution.py:133
  187.8 13.2 %collective-permute-start.4 = (f32[3,8,4,1,128]{4,3,2,1,0:T(1,128)S(1)}, f32[3,8,4,1,128]{4,3,2,1,0:T(1,128)S(1)}, u32[]{:S(2)}, u32[]{:S(2)}) collective-permute-start(f32[3,8,4,1,128]{4,3,2,1,0:T(1,128)S(1)} %get-tuple-element.219), channel_id=1, source_target_pairs={{0,2},{2,4},{4,6},{6,8},{8,10},{10,12},{12,14},{14,16},{16,18},{18... | collective-permute-start | bytes 147464 | tf_op jit(solution)/shard_map/ppermute | solution.py:17
  199.0 5.7 %collective-permute-start.5 = (f32[3,8,4,1,128]{4,3,2,1,0:T(1,128)S(1)}, f32[3,8,4,1,128]{4,3,2,1,0:T(1,128)S(1)}, u32[]{:S(2)}, u32[]{:S(2)}) collective-permute-start(f32[3,8,4,1,128]{4,3,2,1,0:T(1,128)S(1)} %get-tuple-element.220), channel_id=1, source_target_pairs={{2,0},{4,2},{6,4},{8,6},{10,8},{12,10},{14,12},{16,14},{18,16},{20... | collective-permute-start | bytes 147464 | tf_op jit(solution)/shard_map/ppermute | solution.py:20
  205.8 8.3 %collective-permute-start.6 = (f32[3,8,4,10,1]{3,1,4,2,0:T(8,128)S(1)}, f32[3,8,4,10,1]{3,1,4,2,0:T(8,128)S(1)}, u32[]{:S(2)}, u32[]{:S(2)}) collective-permute-start(f32[3,8,4,10,1]{3,1,4,2,0:T(8,128)S(1)} %copy.68), channel_id=1, source_target_pairs={{0,1},{1,0},{2,3},{3,2},{4,5},{5,4},{6,7},{7,6},{8,9},{9,8},{10,11... | collective-permute-start | bytes 11528 | tf_op jit(solution)/shard_map/ppermute | solution.py:17
  211.3 6.3 %collective-permute-start.7 = (f32[3,8,4,10,1]{3,1,4,2,0:T(8,128)S(1)}, f32[3,8,4,10,1]{3,1,4,2,0:T(8,128)S(1)}, u32[]{:S(2)}, u32[]{:S(2)}) collective-permute-start(f32[3,8,4,10,1]{3,1,4,2,0:T(8,128)S(1)} %copy.69), channel_id=1, source_target_pairs={{1,0},{0,1},{3,2},{2,3},{5,4},{4,5},{7,6},{6,7},{9,8},{8,9},{11,10... | collective-permute-start | bytes 11528 | tf_op jit(solution)/shard_map/ppermute | solution.py:20
where the time goes:
time: 223 us; the launch traced here: 221 us
  starting transfers between devices  83.6 us (37%)
  matrix products  55.8 us (25%)
  waiting for transfers between devices  45.7 us (20%)
  local copies, waits for them, and re-layouts  25.4 us (11%)
  other arithmetic  7.53 us (3%)
    dot_general x16, matrix products, visit(): lookup = jnp.einsum('atj,tc->ajc', weights, all_adjoint, precision=highest)  31.3 us
    dot_general x16, matrix products, visit(): products = jnp.einsum('atj,jc->atc', weights, all_number, precision=highest)  22.3 us
    ppermute x4, starting transfers between devices, padded_2(): lax.ppermute(lax.slice_in_dim(block, block.shape[dim] - width, None, axis...  21 us
    all_to_all x1, starting transfers between devices, per_device(): lax.all_to_all(flat_cot, 'sec', split_axis=1, concat_axis=0, tiled=True)  15.7 us
    all_to_all x1, starting transfers between devices, per_device(): lax.all_to_all(flat_number, 'sec', split_axis=1, concat_axis=0, tiled=True)  11.8 us
    ppermute x4, starting transfers between devices, padded_2(): lax.ppermute(lax.slice_in_dim(block, 0, width, axis=dim), axis, backward)  11.6 us
    all_to_all x1, starting transfers between devices, per_device(): lax.all_to_all(cell_adjoint, 'sec', split_axis=0, concat_axis=1, tiled=True)  11.5 us
    all_to_all x1, waiting for transfers between devices, per_device(): lax.all_to_all(cell_coag, 'sec', split_axis=0, concat_axis=1, tiled=True)  11.1 us
  transfers between devices with their start and end apart: 14, of which 7 were waited for; matrix products, arithmetic and copies ran while one was open for 38% of the time, Pallas kernels for 0%

commit v1 on v0

v1 whole, which is shorter than its diff:
```python
import functools

import jax
import jax.numpy as jnp
from jax import lax
from jax.experimental import pallas as pl
from jax.experimental.pallas import tpu as pltpu
from jax.sharding import PartitionSpec as P

step_size = 0.25
vertical_mix = 0.2
highest = lax.Precision.HIGHEST
f32 = jnp.float32
bf16 = jnp.bfloat16

S = 128
B = 16
R = 8
L = 4
X = 8
Y = 128
GROUP = 16
PER = 4

INV, FWD, FWD_PI, BWD, BWD_PI = (256 * i for i in range(5))
FWD_Q, BWD_Q = 1280, 1408
COEF_ROWS = 1536

vmem = pl.BlockSpec(memory_space=pltpu.VMEM)
smem = pl.BlockSpec(memory_space=pltpu.SMEM)


def row_offsets():
    offsets, at = [], 0
    for group in range(S // GROUP):
        offsets.append(at)
        at += GROUP * (S - GROUP * group)
    return offsets, at


OFFSETS, WEIGHT_ROWS = row_offsets()


def call(kernel, outs, in_specs, name, flops=0, nbytes=1 << 20, scratch=(), limit=None):
    single = not isinstance(outs, (tuple, list))
    return pl.pallas_call(
        kernel,
        out_shape=outs,
        in_specs=in_specs,
        out_specs=vmem if single else [vmem] * len(outs),
        scratch_shapes=list(scratch),
        name=name,
        cost_estimate=pl.CostEstimate(flops=flops, bytes_accessed=nbytes, transcendentals=0),
        compiler_params=pltpu.CompilerParams(vmem_limit_bytes=limit or (32 << 20)),
    )


def shape(*dims, dtype=f32):
    return jax.ShapeDtypeStruct(dims, dtype)


def pack_y(tiles):
    lane = lax.broadcasted_iota(jnp.int32, (X, Y), 1)
    packed = jnp.zeros((X, Y), f32)
    for i, tile in enumerate(tiles):
        packed = jnp.where(lane // 2 == i, pltpu.roll(tile, 2 * i + 1, 1), packed)
    return packed


def pack_kernel(n_ref, c_ref, vel_ref, send_ref, low_ref, high_ref, y_ref):
    for m in range(L * X):
        send_ref[pl.ds(m * 16, 8), :] = n_ref[pl.ds(m, R, stride=L * X), :]
        send_ref[pl.ds(m * 16 + 8, 8), :] = c_ref[pl.ds(m, R, stride=L * X), :]
    for ref, row in ((low_ref, 0), (high_ref, X - 1)):
        ref[pl.ds(0, 32), :] = n_ref[pl.ds(row, 32, stride=X), :]
        edge = jnp.concatenate(
            [vel_ref[pl.ds(l * X + row, 1), :] for l in range(L)] + [jnp.zeros((4, Y), f32)], axis=0
        )
        ref[pl.ds(32, 8), :] = edge
    tiles = [n_ref[pl.ds(i * X, X), :] for i in range(R * L)]
    tiles += [vel_ref[pl.ds(32 + l * X, X), :] for l in range(L)]
    y_ref[...] = pack_y(tiles)


def shifted(tile, below, above, packed, i, masks):
    first_row, last_row, first_lane, last_lane = masks
    x_plus = jnp.where(last_row, above, pltpu.roll(tile, X - 1, 0))
    x_minus = jnp.where(first_row, below, pltpu.roll(tile, 1, 0))
    y_plus = jnp.where(last_lane, pltpu.roll(packed, 126 - 2 * i, 1), pltpu.roll(tile, Y - 1, 1))
    low = packed if i == 0 else pltpu.roll(packed, Y - 2 * i, 1)
    y_minus = jnp.where(first_lane, low, pltpu.roll(tile, 1, 1))
    return x_plus, x_minus, y_plus, y_minus


def edge_masks():
    row = lax.broadcasted_iota(jnp.int32, (X, Y), 0)
    lane = lax.broadcasted_iota(jnp.int32, (X, Y), 1)
    return row == 0, row == X - 1, lane == 0, lane == Y - 1


def vertical(column, l):
    return column[min(l + 1, L - 1)] + column[max(l - 1, 0)] - 2.0 * column[l]


def forward_kernel(
    n_ref, below_ref, above_ref, y_ref, vel_ref, rate_ref, factor_ref, diff_ref, local_ref, end_ref
):
    first = lax.axis_index("sec") * R
    masks = edge_masks()
    packed = y_ref[...]
    before = [jnp.zeros((X, Y), f32) for _ in range(L)]
    for s in range(R):
        column = [n_ref[pl.ds((s * L + l) * X, X), :] for l in range(L)]
        diffusion = diff_ref[first + s]
        factor = factor_ref[first + s]
        prior_factor = jnp.where(first + s == 0, 0.0, factor_ref[jnp.maximum(first + s - 1, 0)])
        for l in range(L):
            i = s * L + l
            u = vel_ref[pl.ds(l * X, X), :]
            w = vel_ref[pl.ds(32 + l * X, X), :]
            v = column[l]
            xp, xm, yp, ym = shifted(
                v, below_ref[pl.ds(i, 1), :], above_ref[pl.ds(i, 1), :], packed, i, masks
            )
            moved = (
                -u * (xp - xm) * 0.5
                - w * (yp - ym) * 0.5
                + diffusion * (xp + xm + yp + ym - 4.0 * v)
                + vertical_mix * vertical(column, l)
            )
            rate = rate_ref[pl.ds(l * X, X), :]
            growth = step_size * (rate * factor)
            prior = step_size * (rate * prior_factor)
            value = (v + step_size * moved + prior * before[l]) / (1.0 + growth)
            before[l] = value
            local_ref[pl.ds(i * X, X), :] = value
    for l in range(L):
        end_ref[pl.ds(l * X, X), :] = before[l]


def adjoint_kernel(c_ref, mid_ref, rate_ref, factor_ref, adj_ref, low_ref, high_ref, y_ref):
    first = lax.axis_index("sec") * R
    carried = []
    for l in range(L):
        even = mid_ref[pl.ds(l * 16, 4, stride=4), :]
        odd = mid_ref[pl.ds(l * 16 + 1, 4, stride=4), :]
        carried.append(
            jnp.concatenate(
                [part[k : k + 1] for k in range(4) for part in (even, odd)], axis=0
            )
        )
    tiles = [None] * (R * L)
    for s in reversed(range(R)):
        factor = factor_ref[first + s]
        for l in range(L):
            growth = step_size * (rate_ref[pl.ds(l * X, X), :] * factor)
            value = (c_ref[pl.ds((s * L + l) * X, X), :] + growth * carried[l]) / (1.0 + growth)
            carried[l] = value
            tiles[s * L + l] = value
            adj_ref[pl.ds((s * L + l) * X, X), :] = value
    low_ref[...] = adj_ref[pl.ds(0, 32, stride=X), :]
    high_ref[...] = adj_ref[pl.ds(X - 1, 32, stride=X), :]
    y_ref[...] = pack_y(tiles)


def gradient_kernel(
    adj_ref, below_ref, above_ref, y_ref, vel_ref, vel_below_ref, vel_above_ref, vel_y_ref, diff_ref, out_ref
):
    first = lax.axis_index("sec") * R
    masks = edge_masks()
    packed = y_ref[...]
    winds = []
    for l in range(L):
        u = vel_ref[pl.ds(l * X, X), :]
        w = vel_ref[pl.ds(32 + l * X, X), :]
        edge = (vel_below_ref[pl.ds(32 + l, 1), :], vel_above_ref[pl.ds(32 + l, 1), :])
        up, um, _, _ = shifted(u, *edge, vel_y_ref[...], 32 + l, masks)
        _, _, wp, wm = shifted(w, *edge, vel_y_ref[...], 32 + l, masks)
        winds.append((up * 0.5, um * 0.5, wp * 0.5, wm * 0.5))
    for s in range(R):
        column = [adj_ref[pl.ds((s * L + l) * X, X), :] for l in range(L)]
        diffusion = diff_ref[first + s]
        for l in range(L):
            i = s * L + l
            v = column[l]
            xp, xm, yp, ym = shifted(
                v, below_ref[pl.ds(i, 1), :], above_ref[pl.ds(i, 1), :], packed, i, masks
            )
            up, um, wp, wm = winds[l]
            moved = (
                (up * xp - um * xm)
                + (wp * yp - wm * ym)
                + diffusion * (xp + xm + yp + ym - 4.0 * v)
                + vertical_mix * vertical(column, l)
            )
            out_ref[pl.ds(i * X, X), :] = v + step_size * moved


def final_kernel(back_ref, local_ref, part_ref, next_ref, gradient_ref):
    for s in range(R):
        for l in range(L):
            rows = pl.ds((s * L + l) * X, X)
            next_ref[rows, :] = local_ref[rows, :] + back_ref[pl.ds(l * 128 + s, X, stride=16), :]
            gradient_ref[rows, :] = (
                part_ref[rows, :] + step_size * back_ref[pl.ds(l * 128 + 8 + s, X, stride=16), :]
            )


def weight_kernel(
    kernel_ref, target_ref, factor_ref, rate_ref, weight_ref, turned_ref, coef_ref, rows_ref, column_ref
):
    kernel = kernel_ref[...]
    target = target_ref[...].astype(f32)
    turned = kernel.T
    target_turned = target.T
    turned_ref[...] = turned
    same = target == target_turned
    one = 0.5 * kernel + jnp.where(same, 0.5 * turned, 0.0)
    two = jnp.where(same, 0.0, 0.5 * turned)
    one_high = one.astype(bf16).astype(f32)
    two_high = two.astype(bf16).astype(f32)
    for i, part in enumerate(
        (target, target_turned, one_high, one - one_high, two_high, two - two_high)
    ):
        rows_ref[pl.ds(i * S, S), :] = part

    for group in range(S // GROUP):
        low = group * GROUP
        count = S - low
        ids = (lax.broadcasted_iota(jnp.int32, (count, S), 0) + low).astype(f32)

        def build(k, _, low=low, count=count, ids=ids, start=OFFSETS[group]):
            t1, t2, h1, l1, h2, l2 = (rows_ref[pl.ds(i * S + low + k, 1), :] for i in range(6))
            hit1, hit2 = ids == t1, ids == t2
            high = jnp.where(hit1, h1, jnp.where(hit2, h2, 0.0)).astype(bf16)
            rest = jnp.where(hit1, l1, jnp.where(hit2, l2, 0.0)).astype(bf16)
            rows = pl.ds(pl.multiple_of(start + k * count, 16), count)
            weight_ref[rows, :] = jnp.concatenate([high, rest], axis=1)
            return 0

        lax.fori_loop(0, GROUP, build, 0)

    device = lax.axis_index("sec")
    column_ref[...] = jnp.broadcast_to(factor_ref[...], (S, S)).T
    block = lax.broadcasted_iota(jnp.int32, (B, Y), 0)
    for r in range(2):
        rate = rate_ref[pl.ds(2 * device + r, 1), :]
        growths, inverses = [], []
        for i in range(R):
            growth = step_size * (rate * column_ref[pl.ds(i, B, stride=R), :])
            inverse = 1.0 / (1.0 + growth)
            coef_ref[pl.ds(INV + (i * 2 + r) * B, B), :] = inverse
            growths.append(growth)
            inverses.append(inverse)
        product = None
        for i in range(R):
            if i == 0:
                prior = jnp.where(block == 0, 0.0, pltpu.roll(growths[R - 1], 1, 0))
            else:
                prior = growths[i - 1]
            ratio = prior * inverses[i]
            product = ratio if product is None else ratio * product
            coef_ref[pl.ds(FWD + (i * 2 + r) * B, B), :] = ratio
            coef_ref[pl.ds(FWD_PI + (i * 2 + r) * B, B), :] = product
        q = jnp.where(block == 0, 0.0, product)
        for turn, hop in enumerate((1, 2, 4, 8)):
            coef_ref[pl.ds(FWD_Q + (turn * 2 + r) * B, B), :] = q
            q = q * pltpu.roll(q, hop, 0)
        product = None
        for i in reversed(range(R)):
            ratio = growths[i] * inverses[i]
            product = ratio if product is None else ratio * product
            coef_ref[pl.ds(BWD + (i * 2 + r) * B, B), :] = ratio
            coef_ref[pl.ds(BWD_PI + (i * 2 + r) * B, B), :] = product
        q = jnp.where(block == B - 1, 0.0, product)
        for turn, hop in enumerate((1, 2, 4, 8)):
            coef_ref[pl.ds(BWD_Q + (turn * 2 + r) * B, B), :] = q
            q = q * pltpu.roll(q, B - hop, 0)


def cell_adjoint_kernel(got_ref, coef_ref, end_ref, adj_ref, mid_ref):
    block = lax.broadcasted_iota(jnp.int32, (B, Y), 0)
    for r in range(2):
        value = None
        values = []
        for i in reversed(range(R)):
            at = (i * 2 + r) * B
            source = got_ref[pl.ds(r * 16 + 8 + i, B, stride=32), :] * coef_ref[pl.ds(INV + at, B), :]
            value = source if value is None else source + coef_ref[pl.ds(BWD + at, B), :] * value
            values.append((i, value))
        for turn, hop in enumerate((1, 2, 4, 8)):
            q = coef_ref[pl.ds(BWD_Q + (turn * 2 + r) * B, B), :]
            value = value + q * pltpu.roll(value, B - hop, 0)
        carry = jnp.where(block == B - 1, 0.0, pltpu.roll(value, B - 1, 0))
        for i, local in values:
            full = local + coef_ref[pl.ds(BWD_PI + (i * 2 + r) * B, B), :] * carry
            adj_ref[pl.ds(r * S + i, B, stride=R), :] = full
        mid_ref[pl.ds(r, B, stride=4), :] = carry
        mid_ref[pl.ds(2 + r, B, stride=4), :] = end_ref[pl.ds(r, B, stride=2), :]


def split(value):
    high = value.astype(bf16)
    return high, (value - high.astype(f32)).astype(bf16)


def pair_kernel(
    got_ref, adj_ref, weight_ref, kernel_ref, turned_ref, gain_out, coag_out, n_ref, a_ref, gain_ref, part_ref
):
    for r in range(2):
        for b in range(B):
            n_ref[pl.ds(b * 8, 8), pl.ds(r * Y, Y)] = got_ref[pl.ds(b * 32 + r * 16, 8), :]
        a_ref[:, pl.ds(r * Y, Y)] = adj_ref[pl.ds(r * S, S), :]
    number = n_ref[...]
    high, rest = split(number)
    right = jnp.concatenate([high, high, rest], axis=0)
    gain_ref[...] = jnp.zeros_like(gain_ref)

    for group in range(S // GROUP):
        low = group * GROUP
        count = S - low

        def visit(turn, _, low=low, count=count, start=OFFSETS[group]):
            rows = pl.ds(pl.multiple_of(start + turn * (PER * count), 16), PER * count)
            left = weight_ref[rows, :]
            left = jnp.concatenate([left, left[:, :S]], axis=1)
            found = jnp.dot(left, right, preferred_element_type=f32).reshape(PER, count, 2 * Y)
            total = gain_ref[pl.ds(low, count), :]
            adjoint = a_ref[pl.ds(low, count), :]
            for p in range(PER):
                k = low + turn * PER + p
                total = total + found[p] * n_ref[pl.ds(k, 1), :]
                share = (found[p] * adjoint).reshape(count // 8, 8, 2 * Y).sum(axis=0)
                for r in range(2):
                    rows = pl.ds(pl.multiple_of(r * 8 * S + k * 8, 8), 8)
                    part_ref[rows, :] = share[:, r * Y : (r + 1) * Y]
            gain_ref[pl.ds(low, count), :] = total
            return 0

        lax.fori_loop(0, GROUP // PER, visit, 0)

    adjoint = a_ref[...]
    pull = jnp.dot(kernel_ref[...], number, precision=highest, preferred_element_type=f32)
    back = jnp.dot(turned_ref[...], adjoint * number, precision=highest, preferred_element_type=f32)
    gain = step_size * (0.5 * gain_ref[...] - number * pull)
    for r in range(2):
        gain_out[pl.ds(r * S, S), :] = gain[:, r * Y : (r + 1) * Y]
    other = adjoint * pull + back
    for r in range(2):
        coag = part_ref[pl.ds(r * 8 * S, S, stride=8), :]
        for j in range(1, 8):
            coag = coag + part_ref[pl.ds(r * 8 * S + j, S, stride=8), :]
        coag_out[pl.ds(r * S, S), :] = coag - other[:, r * Y : (r + 1) * Y]


def cell_next_kernel(gain_ref, coag_ref, mid_ref, coef_ref, send_ref):
    block = lax.broadcasted_iota(jnp.int32, (B, Y), 0)
    for r in range(2):
        value = None
        values = []
        for i in range(R):
            at = (i * 2 + r) * B
            source = gain_ref[pl.ds(r * S + i, B, stride=R), :] * coef_ref[pl.ds(INV + at, B), :]
            value = source if value is None else source + coef_ref[pl.ds(FWD + at, B), :] * value
            values.append(value)
        value = value + mid_ref[pl.ds(2 + r, B, stride=4), :]
        for turn, hop in enumerate((1, 2, 4, 8)):
            q = coef_ref[pl.ds(FWD_Q + (turn * 2 + r) * B, B), :]
            value = value + q * pltpu.roll(value, hop, 0)
        carry = jnp.where(block == 0, 0.0, pltpu.roll(value, 1, 0))
        for i in range(R):
            full = values[i] + coef_ref[pl.ds(FWD_PI + (i * 2 + r) * B, B), :] * carry
            send_ref[pl.ds(r * 16 + i, B, stride=32), :] = full
        for b in range(B):
            send_ref[pl.ds(b * 32 + r * 16 + 8, 8), :] = coag_ref[pl.ds(r * S + b * 8, 8), :]


def exchange(rows):
    count = rows.shape[0]
    parts = lax.all_to_all(
        rows.reshape(B, count // B, Y), "sec", split_axis=0, concat_axis=0, tiled=True
    )
    return parts.reshape(count, Y)


def halo(low, high, packed):
    count = lax.axis_size("gx")
    up = [(i, (i + 1) % count) for i in range(count)]
    down = [(target, source) for source, target in up]
    below = lax.ppermute(high, "gx", up)
    above = lax.ppermute(low, "gx", down)
    other = lax.ppermute(packed, "gy", [(0, 1), (1, 0)])
    return below, above, other


def per_device(
    number, cotangent, growth_rate, section_factor, velocity, diffusivity, kernel, target
):
    n = number.reshape(256, Y)
    c = cotangent.reshape(256, Y)
    rate = growth_rate.reshape(32, Y)
    vel = velocity.reshape(64, Y)
    send, low, high, packed = call(
        pack_kernel,
        (shape(512, Y), shape(40, Y), shape(40, Y), shape(X, Y)),
        [vmem] * 3,
        "pack",
    )(n, c, vel)
    got = exchange(send)
    below, above, other = halo(low, high, packed)
    weight, turned, coef = call(
        weight_kernel,
        (shape(WEIGHT_ROWS, 2 * S, dtype=bf16), shape(S, S), shape(COEF_ROWS, Y)),
        [vmem] * 4,
        "weights",
        flops=1 << 20,
        nbytes=6 << 20,
        scratch=(pltpu.VMEM((6 * S, S), f32), pltpu.VMEM((S, S), f32)),
    )(kernel, target, section_factor.reshape(1, S), rate)
    local, ends = call(
        forward_kernel,
        (shape(256, Y), shape(32, Y)),
        [vmem] * 6 + [smem] * 2,
        "forward",
    )(n, below, above, other, vel, rate, section_factor, diffusivity)
    adj, mid = call(
        cell_adjoint_kernel, (shape(256, Y), shape(64, Y)), [vmem] * 3, "cell_adjoint"
    )(got, coef, ends)
    mid_got = exchange(mid)
    gain, coag = call(
        pair_kernel,
        (shape(256, Y), shape(256, Y)),
        [vmem] * 5,
        "pairs",
        flops=1 << 32,
        nbytes=8 << 20,
        scratch=(
            pltpu.VMEM((S, 2 * Y), f32),
            pltpu.VMEM((S, 2 * Y), f32),
            pltpu.VMEM((S, 2 * Y), f32),
            pltpu.VMEM((2 * S * 8, Y), f32),
        ),
    )(got, adj, weight, kernel, turned)
    send_back = call(cell_next_kernel, shape(512, Y), [vmem] * 4, "cell_next")(
        gain, coag, mid_got, coef
    )
    back = exchange(send_back)
    adj_own, a_low, a_high, a_packed = call(
        adjoint_kernel,
        (shape(256, Y), shape(32, Y), shape(32, Y), shape(X, Y)),
        [vmem] * 3 + [smem],
        "adjoint",
    )(c, mid_got, rate, section_factor)
    a_below, a_above, a_other = halo(a_low, a_high, a_packed)
    part = call(gradient_kernel, shape(256, Y), [vmem] * 8 + [smem], "gradient")(
        adj_own, a_below, a_above, a_other, vel, below, above, other, diffusivity
    )
    next_rows, gradient = call(
        final_kernel, (shape(256, Y), shape(256, Y)), [vmem] * 3, "final"
    )(back, local, part)
    return next_rows.reshape(number.shape), gradient.reshape(number.shape)


def solution(mesh):
    return jax.shard_map(
        per_device,
        mesh=mesh,
        in_specs=(
            P("sec", None, "gx", "gy"),
            P("sec", None, "gx", "gy"),
            P(None, "gx", "gy"),
            P(),
            P(None, None, "gx", "gy"),
            P(),
            P(),
            P(),
        ),
        out_specs=(P("sec", None, "gx", "gy"), P("sec", None, "gx", "gy")),
        check_vma=False,
    )
```

time: 223 us -> 98.4 us (0.44)
  the two profiles are of different devices: /device:TPU:1 before, /device:TPU:32 now
where the time goes in v1:
time: 98.4 us; the launch traced here: 97.4 us
  starting transfers between devices  61.6 us (63%)
  Pallas kernels  15.2 us (15%)
  local copies, waits for them, and re-layouts  14.6 us (15%)
  waiting for transfers between devices  5.11 us (5%)
    all_to_all x3, starting transfers between devices, exchange(): lax.all_to_all(rows.reshape(B, count // B, Y), 'sec', split_axis=0, conca...  38.9 us
    unnamed x40, local copies, waits for them, and re-layouts  14.6 us
    ppermute x2, starting transfers between devices, halo(): above = lax.ppermute(low, 'gx', down)  11.5 us
    pallas_call x1, Pallas kernels, per_device(): call(pair_kernel, (shape(256, Y), shape(256, Y)), [vmem] * 5, 'pairs', fl...  7.93 us
    ppermute x2, starting transfers between devices, halo(): other = lax.ppermute(packed, 'gy', [(0, 1), (1, 0)])  7.34 us
    ppermute x2, waiting for transfers between devices, halo(): other = lax.ppermute(packed, 'gy', [(0, 1), (1, 0)])  4.76 us
    ppermute x2, starting transfers between devices, halo(): below = lax.ppermute(high, 'gx', up)  3.83 us
  transfers between devices with their start and end apart: 9, of which 2 were waited for; matrix products, arithmetic and copies ran while one was open for 0% of the time, Pallas kernels for 12%

profile of v1, /device:TPU:32, one launch (start us, length us, event | category | flops | bytes accessed | tf_op | source)
XLA Modules:
  0.0 97.4 jit_solution(216978034014423190)
XLA Ops:
  0.6 0.0 copy-start
  0.6 0.9 copy-done
  1.5 0.0 copy-start.2
  1.5 0.9 copy-done.2
  2.4 0.0 copy-start.4
  2.4 0.8 copy-done.4
  3.2 0.9 pack.1
  4.1 15.2 %all-to-all-start = ((f32[16,32,128]{2,1,0:T(8,128)}), f32[16,32,128]{2,1,0:T(8,128)S(1)}, u32[]{:S(2)}, u32[]{:S(2)}) async-start(f32[16,32,128]{2,1,0:T(8,128)} %bitcast.3), calls=%async_computation | async-start | bytes 524288 | tf_op jit(solution)/shard_map/all_to_all | solution.py:380
  19.3 1.9 %collective-permute-start = (f32[40,128]{1,0:T(8,128)S(1)}, f32[40,128]{1,0:T(8,128)S(1)}, u32[]{:S(2)}, u32[]{:S(2)}) collective-permute-start(f32[40,128]{1,0:T(8,128)S(1)} %get-tuple-element.23), channel_id=1, source_target_pairs={{0,2},{2,4},{4,6},{6,8},{8,10},{10,12},{12,14},{14,16},{16,18},{18... | collective-permute-start | bytes 61448 | tf_op jit(solution)/shard_map/ppermute | solution.py:390
  21.2 5.8 %collective-permute-start.1 = (f32[40,128]{1,0:T(8,128)S(1)}, f32[40,128]{1,0:T(8,128)S(1)}, u32[]{:S(2)}, u32[]{:S(2)}) collective-permute-start(f32[40,128]{1,0:T(8,128)S(1)} %get-tuple-element.24), channel_id=1, source_target_pairs={{2,0},{4,2},{6,4},{8,6},{10,8},{12,10},{14,12},{16,14},{18,16},{20... | collective-permute-start | bytes 61448 | tf_op jit(solution)/shard_map/ppermute | solution.py:391
  27.0 5.1 %collective-permute-start.2 = (f32[8,128]{1,0:T(8,128)S(1)}, f32[8,128]{1,0:T(8,128)S(1)}, u32[]{:S(2)}, u32[]{:S(2)}) collective-permute-start(f32[8,128]{1,0:T(8,128)S(1)} %get-tuple-element.25), channel_id=1, source_target_pairs={{0,1},{1,0},{2,3},{3,2},{4,5},{5,4},{6,7},{7,6},{8,9},{9,8},{10,11... | collective-permute-start | bytes 12296 | tf_op jit(solution)/shard_map/ppermute | solution.py:392
  32.1 0.0 copy-start.7
  32.1 0.7 copy-done.7
  32.8 0.0 copy-start.10
  32.8 0.8 copy-done.10
  33.6 0.0 copy-start.11
  33.6 0.8 copy-done.11
  34.5 0.0 copy-start.13
  34.5 0.7 copy-done.13
  35.1 1.8 %weights.1 = (bf16[9216,256]{1,0:T(8,128)(2,1)S(1)}, f32[128,128]{1,0:T(8,128)S(1)}, f32[1536,128]{1,0:T(8,128)S(1)}) custom-call(f32[128,128]{1,0:T(8,128)S(1)} %copy-done.11, s32[128,128]{1,0:T(8,128)S(1)} %copy-done.10, f32[1,128]{1,0:T(1,128)S(1)} %bitcast.28, f32[32,128]{1,0:T(8,128)S(1)} %bitcast.25), custom_call_target="tpu_custom_call" | custom-call | flops 1048576 | bytes 6291456 | tf_op jit(solution)/shard_map/weights/pallas_call | solution.py:411
  37.0 0.0 copy-start.18
  37.0 2.1 %copy-done.18 = bf16[9216,256]{1,0:T(8,128)(2,1)} copy-done((bf16[9216,256]{1,0:T(8,128)(2,1)}, bf16[9216,256]{1,0:T(8,128)(2,1)S(1)}, u32[]{:S(2)}) %copy-start.18) | copy-done | bytes 4718616
  39.1 0.0 collective-permute-done.2.y_ref.vel_y_ref
  39.1 0.0 collective-permute-done.below_ref.vel_below_ref
  39.1 0.0 collective-permute-done.1.above_ref.vel_above_ref
  39.1 0.0 copy-start.1
  39.2 0.9 copy-done.1
  40.1 0.8 copy-done.5
  40.8 0.0 copy-start.8
  40.8 0.7 copy-done.8
  41.5 0.0 copy-start.14
  41.5 0.7 copy-done.14
  42.2 0.0 copy-start.16
  42.2 0.7 copy-done.16
  42.8 0.7 forward.1
  43.6 0.0 all-to-all-done
  43.6 0.7 cell_adjoint.1
  44.3 12.0 %all-to-all-start.1 = ((f32[16,4,128]{2,1,0:T(4,128)}), f32[16,4,128]{2,1,0:T(4,128)S(1)}, u32[]{:S(2)}, u32[]{:S(2)}) async-start(f32[16,4,128]{2,1,0:T(4,128)} %bitcast.7), calls=%async_computation.1 | async-start | bytes 65536 | tf_op jit(solution)/shard_map/all_to_all | solution.py:380
  56.3 0.0 copy-start.12
  56.4 0.8 copy-done.12
  57.2 0.0 copy-start.19
  57.2 2.3 %copy-done.19 = bf16[9216,256]{1,0:T(8,128)(2,1)S(1)} copy-done((bf16[9216,256]{1,0:T(8,128)(2,1)S(1)}, bf16[9216,256]{1,0:T(8,128)(2,1)}, u32[]{:S(2)}) %copy-start.19) | copy-done | bytes 4718616
  59.5 0.0 copy-start.3
  59.5 0.0 copy-start.9
  59.5 0.0 copy-start.17
  59.5 7.9 %pairs.1 = (f32[256,128]{1,0:T(8,128)S(1)}, f32[256,128]{1,0:T(8,128)S(1)}) custom-call(f32[512,128]{1,0:T(8,128)S(1)} %bitcast.15, f32[256,128]{1,0:T(8,128)S(1)} %get-tuple-element.27.adj_ref, bf16[9216,256]{1,0:T(8,128)(2,1)S(1)} %copy-done.19, f32[128,128]{1,0:T(8,128)S(1)} %copy-done.12, f32[128,128]{1,0:T(8,128)S(1)} %get-tuple-element.29.turned_ref), custom_call_target="tpu_custom_call" | custom-call | flops 4294967296 | bytes 8388608 | tf_op jit(solution)/shard_map/pairs/pallas_call | solution.py:430
  67.5 0.3 all-to-all-done.1
  67.8 0.9 cell_next.1
  68.7 11.7 %all-to-all-start.2 = ((f32[16,32,128]{2,1,0:T(8,128)}), f32[16,32,128]{2,1,0:T(8,128)S(1)}, u32[]{:S(2)}, u32[]{:S(2)}) async-start(f32[16,32,128]{2,1,0:T(8,128)} %bitcast.9), calls=%async_computation.2 | async-start | bytes 524288 | tf_op jit(solution)/shard_map/all_to_all | solution.py:380
  80.4 0.0 copy-done.3
  80.4 0.0 copy-done.9
  80.4 0.0 copy-done.15
  80.4 0.7 adjoint.1
  81.1 1.9 %collective-permute-start.3 = (f32[32,128]{1,0:T(8,128)S(1)}, f32[32,128]{1,0:T(8,128)S(1)}, u32[]{:S(2)}, u32[]{:S(2)}) collective-permute-start(f32[32,128]{1,0:T(8,128)S(1)} %get-tuple-element.35), channel_id=1, source_target_pairs={{0,2},{2,4},{4,6},{6,8},{8,10},{10,12},{12,14},{14,16},{16,18},{18... | collective-permute-start | bytes 49160 | tf_op jit(solution)/shard_map/ppermute | solution.py:390
  83.0 5.8 %collective-permute-start.4 = (f32[32,128]{1,0:T(8,128)S(1)}, f32[32,128]{1,0:T(8,128)S(1)}, u32[]{:S(2)}, u32[]{:S(2)}) collective-permute-start(f32[32,128]{1,0:T(8,128)S(1)} %get-tuple-element.36), channel_id=1, source_target_pairs={{2,0},{4,2},{6,4},{8,6},{10,8},{12,10},{14,12},{16,14},{18,16},{20... | collective-permute-start | bytes 49160 | tf_op jit(solution)/shard_map/ppermute | solution.py:391
  88.8 2.2 %collective-permute-start.5 = (f32[8,128]{1,0:T(8,128)S(1)}, f32[8,128]{1,0:T(8,128)S(1)}, u32[]{:S(2)}, u32[]{:S(2)}) collective-permute-start(f32[8,128]{1,0:T(8,128)S(1)} %get-tuple-element.37), channel_id=1, source_target_pairs={{0,1},{1,0},{2,3},{3,2},{4,5},{5,4},{6,7},{7,6},{8,9},{9,8},{10,11... | collective-permute-start | bytes 12296 | tf_op jit(solution)/shard_map/ppermute | solution.py:392
  91.0 4.8 %collective-permute-done.5.y_ref = f32[8,128]{1,0:T(8,128)S(1)} collective-permute-done((f32[8,128]{1,0:T(8,128)S(1)}, f32[8,128]{1,0:T(8,128)S(1)}, u32[]{:S(2)}, u32[]{:S(2)}) %collective-permute-start.5) | collective-permute-done | bytes 4128 | tf_op jit(solution)/shard_map/ppermute | solution.py:392
  95.8 0.0 collective-permute-done.3.below_ref
  95.8 0.0 collective-permute-done.4.above_ref
  95.8 0.0 copy-done.6
  95.8 0.0 copy-done.17
  95.8 0.8 gradient.1.part_ref
  96.6 0.0 all-to-all-done.2
  96.6 0.8 final.1
  (3 shorter events, 0.0 us)
Async XLA Ops:
  0.6 0.9 copy-start
  1.5 0.9 copy-start.2
  2.4 0.8 copy-start.4
  4.1 39.5 %all-to-all-start = ((f32[16,32,128]{2,1,0:T(8,128)}), f32[16,32,128]{2,1,0:T(8,128)S(1)}, u32[]{:S(2)}, u32[]{:S(2)}) async-start(f32[16,32,128]{2,1,0:T(8,128)} %bitcast.3), calls=%async_computation | async-start | bytes 524288 | tf_op jit(solution)/shard_map/all_to_all | solution.py:380
  19.3 19.8 %collective-permute-start = (f32[40,128]{1,0:T(8,128)S(1)}, f32[40,128]{1,0:T(8,128)S(1)}, u32[]{:S(2)}, u32[]{:S(2)}) collective-permute-start(f32[40,128]{1,0:T(8,128)S(1)} %get-tuple-element.23), channel_id=1, source_target_pairs={{0,2},{2,4},{4,6},{6,8},{8,10},{10,12},{12,14},{14,16},{16,18},{18... | collective-permute-start | bytes 61448 | tf_op jit(solution)/shard_map/ppermute | solution.py:390
  21.2 17.9 %collective-permute-start.1 = (f32[40,128]{1,0:T(8,128)S(1)}, f32[40,128]{1,0:T(8,128)S(1)}, u32[]{:S(2)}, u32[]{:S(2)}) collective-permute-start(f32[40,128]{1,0:T(8,128)S(1)} %get-tuple-element.24), channel_id=1, source_target_pairs={{2,0},{4,2},{6,4},{8,6},{10,8},{12,10},{14,12},{16,14},{18,16},{20... | collective-permute-start | bytes 61448 | tf_op jit(solution)/shard_map/ppermute | solution.py:391
  27.0 12.2 %collective-permute-start.2 = (f32[8,128]{1,0:T(8,128)S(1)}, f32[8,128]{1,0:T(8,128)S(1)}, u32[]{:S(2)}, u32[]{:S(2)}) collective-permute-start(f32[8,128]{1,0:T(8,128)S(1)} %get-tuple-element.25), channel_id=1, source_target_pairs={{0,1},{1,0},{2,3},{3,2},{4,5},{5,4},{6,7},{7,6},{8,9},{9,8},{10,11... | collective-permute-start | bytes 12296 | tf_op jit(solution)/shard_map/ppermute | solution.py:392
  32.1 0.7 copy-start.7
  32.8 0.8 copy-start.10
  33.6 0.8 copy-start.11
  34.5 0.7 copy-start.13
  37.0 2.2 %copy-start.18 = (bf16[9216,256]{1,0:T(8,128)(2,1)}, bf16[9216,256]{1,0:T(8,128)(2,1)S(1)}, u32[]{:S(2)}) copy-start(bf16[9216,256]{1,0:T(8,128)(2,1)S(1)} %get-tuple-element.28.weight_ref) | copy-start | bytes 14155780
  39.1 0.9 copy-start.1
  40.1 0.8 copy-start.5
  40.8 0.7 copy-start.8
  41.5 0.7 copy-start.14
  42.2 0.7 copy-start.16
  44.3 23.5 %all-to-all-start.1 = ((f32[16,4,128]{2,1,0:T(4,128)}), f32[16,4,128]{2,1,0:T(4,128)S(1)}, u32[]{:S(2)}, u32[]{:S(2)}) async-start(f32[16,4,128]{2,1,0:T(4,128)} %bitcast.7), calls=%async_computation.1 | async-start | bytes 65536 | tf_op jit(solution)/shard_map/all_to_all | solution.py:380
  56.3 0.8 copy-start.12
  57.2 2.3 %copy-start.19 = (bf16[9216,256]{1,0:T(8,128)(2,1)S(1)}, bf16[9216,256]{1,0:T(8,128)(2,1)}, u32[]{:S(2)}) copy-start(bf16[9216,256]{1,0:T(8,128)(2,1)} %copy-done.18) | copy-start | bytes 14155780
  59.5 20.9 %copy-start.3 = (f32[8,4,8,128]{3,2,1,0:T(8,128)S(1)}, f32[8,4,8,128]{3,2,1,0:T(8,128)}, u32[]{:S(2)}) copy-start(f32[8,4,8,128]{3,2,1,0:T(8,128)} %param.9) | copy-start | bytes 393220
  59.5 20.9 %copy-start.9 = (f32[4,8,128]{2,1,0:T(8,128)S(1)}, f32[4,8,128]{2,1,0:T(8,128)}, u32[]{:S(2)}) copy-start(f32[4,8,128]{2,1,0:T(8,128)} %param.10) | copy-start | bytes 49156
  59.5 20.9 %copy-start.15 = (f32[128]{0:T(128)S(1)}, f32[128]{0:T(128)}, u32[]{:S(2)}) copy-start(f32[128]{0:T(128)} %factor_ref.3) | copy-start | bytes 1540
  59.5 36.3 %copy-start.6 = (f32[2,4,8,128]{3,2,1,0:T(8,128)S(1)}, f32[2,4,8,128]{3,2,1,0:T(8,128)}, u32[]{:S(2)}) copy-start(f32[2,4,8,128]{3,2,1,0:T(8,128)} %param.12) | copy-start | bytes 98308
  59.5 36.3 %copy-start.17 = (f32[128]{0:T(128)S(1)}, f32[128]{0:T(128)}, u32[]{:S(2)}) copy-start(f32[128]{0:T(128)} %diff_ref.3) | copy-start | bytes 1540
  68.7 27.9 %all-to-all-start.2 = ((f32[16,32,128]{2,1,0:T(8,128)}), f32[16,32,128]{2,1,0:T(8,128)S(1)}, u32[]{:S(2)}, u32[]{:S(2)}) async-start(f32[16,32,128]{2,1,0:T(8,128)} %bitcast.9), calls=%async_computation.2 | async-start | bytes 524288 | tf_op jit(solution)/shard_map/all_to_all | solution.py:380
  81.1 14.7 %collective-permute-start.3 = (f32[32,128]{1,0:T(8,128)S(1)}, f32[32,128]{1,0:T(8,128)S(1)}, u32[]{:S(2)}, u32[]{:S(2)}) collective-permute-start(f32[32,128]{1,0:T(8,128)S(1)} %get-tuple-element.35), channel_id=1, source_target_pairs={{0,2},{2,4},{4,6},{6,8},{8,10},{10,12},{12,14},{14,16},{16,18},{18... | collective-permute-start | bytes 49160 | tf_op jit(solution)/shard_map/ppermute | solution.py:390
  83.0 12.8 %collective-permute-start.4 = (f32[32,128]{1,0:T(8,128)S(1)}, f32[32,128]{1,0:T(8,128)S(1)}, u32[]{:S(2)}, u32[]{:S(2)}) collective-permute-start(f32[32,128]{1,0:T(8,128)S(1)} %get-tuple-element.36), channel_id=1, source_target_pairs={{2,0},{4,2},{6,4},{8,6},{10,8},{12,10},{14,12},{16,14},{18,16},{20... | collective-permute-start | bytes 49160 | tf_op jit(solution)/shard_map/ppermute | solution.py:391
  88.8 7.0 %collective-permute-start.5 = (f32[8,128]{1,0:T(8,128)S(1)}, f32[8,128]{1,0:T(8,128)S(1)}, u32[]{:S(2)}, u32[]{:S(2)}) collective-permute-start(f32[8,128]{1,0:T(8,128)S(1)} %get-tuple-element.37), channel_id=1, source_target_pairs={{0,1},{1,0},{2,3},{3,2},{4,5},{5,4},{6,7},{7,6},{8,9},{9,8},{10,11... | collective-permute-start | bytes 12296 | tf_op jit(solution)/shard_map/ppermute | solution.py:392

commit v2 on v0

v2 whole, which is shorter than its diff:
```python
import jax
import jax.numpy as jnp
from jax import lax
from jax.experimental import pallas as pl
from jax.experimental.pallas import tpu as pltpu
from jax.sharding import PartitionSpec as P

step_size = 0.25
vertical_mix = 0.2
highest = lax.Precision.HIGHEST
f32 = jnp.float32
bf16 = jnp.bfloat16

S = 128
B = 16
R = 8
L = 4
X = 8
Y = 128
GROUP = 16
PER = 4

INV, FWD, FWD_PI = (256 * i for i in range(3))
FWD_Q = 768
COEF_ROWS = 896
EDGE_ROWS = S + 8

vmem = pl.BlockSpec(memory_space=pltpu.VMEM)
hbm = pl.BlockSpec(memory_space=pltpu.HBM)


def row_offsets():
    offsets, at = [], 0
    for group in range(S // GROUP):
        offsets.append(at)
        at += GROUP * (S - GROUP * group)
    return offsets, at


OFFSETS, WEIGHT_ROWS = row_offsets()


def call(kernel, outs, in_specs, name, flops=0, nbytes=1 << 20, scratch=(), limit=None):
    single = not isinstance(outs, (tuple, list))
    return pl.pallas_call(
        kernel,
        out_shape=outs,
        in_specs=in_specs,
        out_specs=vmem if single else [vmem] * len(outs),
        scratch_shapes=list(scratch),
        name=name,
        cost_estimate=pl.CostEstimate(flops=flops, bytes_accessed=nbytes, transcendentals=0),
        compiler_params=pltpu.CompilerParams(vmem_limit_bytes=limit or (32 << 20)),
    )


def shape(*dims, dtype=f32):
    return jax.ShapeDtypeStruct(dims, dtype)


def swap_groups(tiles):
    group = lax.broadcasted_iota(jnp.int32, (8, Y), 1) // 8
    tiles = list(tiles)
    for bit in (1, 2, 4, 8):
        upper = (group & bit) != 0
        for i in range(B):
            if i & bit == 0:
                a, b = tiles[i], tiles[i | bit]
                tiles[i] = jnp.where(upper, pltpu.roll(b, 8 * bit, 1), a)
                tiles[i | bit] = jnp.where(upper, b, pltpu.roll(a, Y - 8 * bit, 1))
    return tiles


def own_cells(rows, device):
    shift = lax.rem(Y - 8 * device, Y)
    moved = pltpu.roll(pltpu.roll(rows, shift, 1), 0, 1, stride=8, stride_axis=0)
    group = lax.broadcasted_iota(jnp.int32, (B, Y), 1) // 8
    row = lax.broadcasted_iota(jnp.int32, (B, Y), 0)
    return jnp.sum(jnp.where(group == row, moved, 0.0), axis=0, keepdims=True)


def pack_kernel(
    n_hbm, c_hbm, rate_hbm, vel_hbm, factor_hbm, diff_hbm, kernel_hbm, target_hbm,
    send_ref, own_ref, factor_ref, diff_ref, kernel_ref, target_ref,
    n_ref, c_ref, rate_ref, vel_ref, row_ref, sems,
):
    device = lax.axis_index("sec")
    pairs = (
        (n_hbm, n_ref),
        (c_hbm, c_ref),
        (rate_hbm, rate_ref),
        (vel_hbm, vel_ref),
        (factor_hbm, row_ref.at[pl.ds(0, 1)]),
        (diff_hbm, row_ref.at[pl.ds(8, 1)]),
        (kernel_hbm, kernel_ref),
        (target_hbm, target_ref),
    )
    copies = [pltpu.make_async_copy(a, b, sems.at[i]) for i, (a, b) in enumerate(pairs)]
    for copy in copies:
        copy.start()
    for array, ref in enumerate((n_ref, c_ref)):
        copies[array].wait()
        for half in range(2):
            tiles = swap_groups(
                ref[pl.ds(half * 16 + g, R, stride=L * X), :] for g in range(B)
            )
            for d, tile in enumerate(tiles):
                send_ref[pl.ds(d * 32 + array * 16 + half * 8, 8), :] = tile
    for copy in copies[2:]:
        copy.wait()
    rows = [own_cells(rate_ref[pl.ds(h * 16, 16), :], device) for h in range(2)]
    rows += [own_cells(vel_ref[pl.ds(h * 16, 16), :], device) for h in range(4)]
    own_ref[...] = jnp.concatenate(rows + [jnp.zeros((2, Y), f32)], axis=0)
    factor_ref[...] = jnp.broadcast_to(row_ref[pl.ds(0, 1), :], (S, S)).T
    diff_ref[...] = jnp.broadcast_to(row_ref[pl.ds(8, 1), :], (S, S)).T


def lane_parts():
    lane = lax.broadcasted_iota(jnp.int32, (8, Y), 1)
    return lane // 64, (lane // 8) % 8, lane % 8


def turn(tile, shift):
    shift = shift % Y
    return tile if shift == 0 else pltpu.roll(tile, shift, 1)


def pack_edges(tiles, which, refs, rows):
    _, x, y = which
    x_up, x_down, y_up, y_down = (jnp.zeros((8, Y), f32) for _ in range(4))
    for i, tile in enumerate(tiles):
        x_up = jnp.where(x == i, turn(tile, 8 * (i - 7)), x_up)
        x_down = jnp.where(x == 7 - i, turn(tile, 8 * (7 - i)), x_down)
        y_up = jnp.where(y == i, turn(tile, i - 7), y_up)
        y_down = jnp.where(y == 7 - i, turn(tile, 7 - i), y_down)
    for ref, edge in zip(refs, (x_up, x_down, y_up, y_down)):
        ref[rows, :] = edge


def shifted(tile, edges, i, which):
    _, x, y = which
    from_low_x, from_high_x, from_low_y, from_high_y = edges
    x_minus = jnp.where(x == 0, turn(from_low_x, -8 * i), turn(tile, 8))
    x_plus = jnp.where(x == 7, turn(from_high_x, 8 * i), turn(tile, -8))
    y_minus = jnp.where(y == 0, turn(from_low_y, -i), turn(tile, 1))
    y_plus = jnp.where(y == 7, turn(from_high_y, i), turn(tile, -1))
    return x_plus, x_minus, y_plus, y_minus


def vertical(low, high, which):
    first = which[0] == 0
    a, b = turn(low, 64), turn(high, 64)
    return (
        a + jnp.where(first, low, b) - 2.0 * low,
        b + jnp.where(first, a, high) - 2.0 * high,
    )


def adjoint_kernel(
    got_ref, own_ref, factor_ref, adj_ref, coef_ref, x_up_ref, x_down_ref, y_up_ref, y_down_ref
):
    block = lax.broadcasted_iota(jnp.int32, (B, Y), 0)
    for h in range(2):
        rate = own_ref[pl.ds(h, 1), :]
        growths, inverses = [], []
        for i in range(R):
            growth = step_size * (rate * factor_ref[pl.ds(i, B, stride=R), :])
            inverse = 1.0 / (1.0 + growth)
            coef_ref[pl.ds(INV + (i * 2 + h) * B, B), :] = inverse
            growths.append(growth)
            inverses.append(inverse)
        product = None
        for i in range(R):
            prior = growths[i - 1] if i else jnp.where(block == 0, 0.0, pltpu.roll(growths[R - 1], 1, 0))
            ratio = prior * inverses[i]
            product = ratio if product is None else ratio * product
            coef_ref[pl.ds(FWD + (i * 2 + h) * B, B), :] = ratio
            coef_ref[pl.ds(FWD_PI + (i * 2 + h) * B, B), :] = product
        q = jnp.where(block == 0, 0.0, product)
        for turns, hop in enumerate((1, 2, 4, 8)):
            coef_ref[pl.ds(FWD_Q + (turns * 2 + h) * B, B), :] = q
            q = q * pltpu.roll(q, hop, 0)
        value, product, values = None, None, []
        for i in reversed(range(R)):
            source = got_ref[pl.ds(16 + h * 8 + i, B, stride=32), :] * inverses[i]
            ratio = growths[i] * inverses[i]
            value = source if value is None else source + ratio * value
            product = ratio if product is None else ratio * product
            values.append((i, value, product))
        q = jnp.where(block == B - 1, 0.0, product)
        for hop in (1, 2, 4, 8):
            value = value + q * pltpu.roll(value, B - hop, 0)
            q = q * pltpu.roll(q, B - hop, 0)
        carry = jnp.where(block == B - 1, 0.0, pltpu.roll(value, B - 1, 0))
        for i, local, product in values:
            adj_ref[pl.ds(h * S + i, B, stride=R), :] = local + product * carry
    which = lane_parts()
    refs = (x_up_ref, x_down_ref, y_up_ref, y_down_ref)
    for b in range(B):
        tiles = [got_ref[pl.ds(b * 32 + h * 8, 8), :] for h in range(2)]
        tiles += [adj_ref[pl.ds(h * S + b * 8, 8), :] for h in range(2)]
        pack_edges(tiles, which, refs, pl.ds(b * 8, 8))
    winds = [jnp.broadcast_to(own_ref[pl.ds(2 + h, 1), :], (8, Y)) for h in range(4)]
    pack_edges(winds, which, refs, pl.ds(S, 8))


def split(value):
    high = value.astype(bf16)
    return high, (value - high.astype(f32)).astype(bf16)


def pair_kernel(
    got_ref, adj_ref, kernel_ref, target_ref, gain_out, coag_out,
    n_ref, a_ref, gain_ref, part_ref, weight_ref, rows_ref,
):
    kernel = kernel_ref[...]
    target = target_ref[...].astype(f32)
    turned = kernel.T
    target_turned = target.T
    same = target == target_turned
    one = 0.5 * kernel + jnp.where(same, 0.5 * turned, 0.0)
    two = jnp.where(same, 0.0, 0.5 * turned)
    one_high = one.astype(bf16).astype(f32)
    two_high = two.astype(bf16).astype(f32)
    for i, part in enumerate(
        (target, target_turned, one_high, one - one_high, two_high, two - two_high)
    ):
        rows_ref[pl.ds(i * S, S), :] = part

    for group in range(S // GROUP):
        low = group * GROUP
        count = S - low
        ids = (lax.broadcasted_iota(jnp.int32, (count, S), 0) + low).astype(f32)

        def build(k, _, low=low, count=count, ids=ids, start=OFFSETS[group]):
            t1, t2, h1, l1, h2, l2 = (rows_ref[pl.ds(i * S + low + k, 1), :] for i in range(6))
            hit1, hit2 = ids == t1, ids == t2
            high = jnp.where(hit1, h1, jnp.where(hit2, h2, 0.0)).astype(bf16)
            rest = jnp.where(hit1, l1, jnp.where(hit2, l2, 0.0)).astype(bf16)
            rows = pl.ds(pl.multiple_of(start + k * count, 16), count)
            weight_ref[rows, :] = jnp.concatenate([high, rest], axis=1)
            return 0

        lax.fori_loop(0, GROUP, build, 0)

    for r in range(2):
        for b in range(B):
            n_ref[pl.ds(b * 8, 8), pl.ds(r * Y, Y)] = got_ref[pl.ds(b * 32 + r * 8, 8), :]
        a_ref[:, pl.ds(r * Y, Y)] = adj_ref[pl.ds(r * S, S), :]
    number = n_ref[...]
    high, rest = split(number)
    right = jnp.concatenate([high, high, rest], axis=0)
    gain_ref[...] = jnp.zeros_like(gain_ref)

    for group in range(S // GROUP):
        low = group * GROUP
        count = S - low

        def visit(turns, _, low=low, count=count, start=OFFSETS[group]):
            rows = pl.ds(pl.multiple_of(start + turns * (PER * count), 16), PER * count)
            left = weight_ref[rows, :]
            left = jnp.concatenate([left, left[:, :S]], axis=1)
            found = jnp.dot(left, right, preferred_element_type=f32).reshape(PER, count, 2 * Y)
            total = gain_ref[pl.ds(low, count), :]
            adjoint = a_ref[pl.ds(low, count), :]
            for p in range(PER):
                k = low + turns * PER + p
                total = total + found[p] * n_ref[pl.ds(k, 1), :]
                share = (found[p] * adjoint).reshape(count // 8, 8, 2 * Y).sum(axis=0)
                for r in range(2):
                    rows = pl.ds(pl.multiple_of(r * 8 * S + k * 8, 8), 8)
                    part_ref[rows, :] = share[:, r * Y : (r + 1) * Y]
            gain_ref[pl.ds(low, count), :] = total
            return 0

        lax.fori_loop(0, GROUP // PER, visit, 0)

    adjoint = a_ref[...]
    pull = jnp.dot(kernel, number, precision=highest, preferred_element_type=f32)
    back = jnp.dot(turned, adjoint * number, precision=highest, preferred_element_type=f32)
    gain = step_size * (0.5 * gain_ref[...] - number * pull)
    for r in range(2):
        gain_out[pl.ds(r * S, S), :] = gain[:, r * Y : (r + 1) * Y]
    other = adjoint * pull + back
    for r in range(2):
        coag = part_ref[pl.ds(r * 8 * S, S, stride=8), :]
        for j in range(1, 8):
            coag = coag + part_ref[pl.ds(r * 8 * S + j, S, stride=8), :]
        coag_out[pl.ds(r * S, S), :] = coag - other[:, r * Y : (r + 1) * Y]


def next_kernel(
    got_ref, adj_ref, own_ref, diff_ref, coef_ref, gain_ref, coag_ref,
    low_x_ref, high_x_ref, low_y_ref, high_y_ref, send_ref, right_ref,
):
    which = lane_parts()
    refs = (low_x_ref, high_x_ref, low_y_ref, high_y_ref)
    wind_edges = [ref[pl.ds(S, 8), :] for ref in refs]
    winds = []
    for h in range(2):
        u = jnp.broadcast_to(own_ref[pl.ds(2 + h, 1), :], (8, Y))
        w = jnp.broadcast_to(own_ref[pl.ds(4 + h, 1), :], (8, Y))
        up, um, _, _ = shifted(u, wind_edges, h, which)
        _, _, wp, wm = shifted(w, wind_edges, 2 + h, which)
        winds.append((0.5 * u, 0.5 * w, 0.5 * up, 0.5 * um, 0.5 * wp, 0.5 * wm))
    for b in range(B):
        edges = [ref[pl.ds(b * 8, 8), :] for ref in refs]
        diffusion = diff_ref[pl.ds(b * 8, 8), :]
        numbers = [got_ref[pl.ds(b * 32 + h * 8, 8), :] for h in range(2)]
        adjoints = [adj_ref[pl.ds(h * S + b * 8, 8), :] for h in range(2)]
        number_levels = vertical(*numbers, which)
        adjoint_levels = vertical(*adjoints, which)
        for h in range(2):
            u, w, up, um, wp, wm = winds[h]
            rows = pl.ds(h * S + b * 8, 8)
            v = numbers[h]
            xp, xm, yp, ym = shifted(v, edges, h, which)
            moved = (
                diffusion * (xp + xm + yp + ym - 4.0 * v)
                - u * (xp - xm)
                - w * (yp - ym)
                + vertical_mix * number_levels[h]
            )
            right_ref[rows, :] = v + step_size * moved + gain_ref[rows, :]
            v = adjoints[h]
            xp, xm, yp, ym = shifted(v, edges, 2 + h, which)
            moved = (
                diffusion * (xp + xm + yp + ym - 4.0 * v)
                + (up * xp - um * xm)
                + (wp * yp - wm * ym)
                + vertical_mix * adjoint_levels[h]
            )
            send_ref[pl.ds(b * 32 + 16 + h * 8, 8), :] = v + step_size * (moved + coag_ref[rows, :])
    block = lax.broadcasted_iota(jnp.int32, (B, Y), 0)
    for h in range(2):
        value, values = None, []
        for i in range(R):
            at = (i * 2 + h) * B
            source = right_ref[pl.ds(h * S + i, B, stride=R), :] * coef_ref[pl.ds(INV + at, B), :]
            value = source if value is None else source + coef_ref[pl.ds(FWD + at, B), :] * value
            values.append(value)
        for turns, hop in enumerate((1, 2, 4, 8)):
            q = coef_ref[pl.ds(FWD_Q + (turns * 2 + h) * B, B), :]
            value = value + q * pltpu.roll(value, hop, 0)
        carry = jnp.where(block == 0, 0.0, pltpu.roll(value, 1, 0))
        for i in range(R):
            full = values[i] + coef_ref[pl.ds(FWD_PI + (i * 2 + h) * B, B), :] * carry
            send_ref[pl.ds(h * 8 + i, B, stride=32), :] = full


def unpack_kernel(back_ref, next_ref, gradient_ref):
    for array, ref in enumerate((next_ref, gradient_ref)):
        for half in range(2):
            tiles = swap_groups(
                back_ref[pl.ds(d * 32 + array * 16 + half * 8, 8), :] for d in range(B)
            )
            for g, tile in enumerate(tiles):
                ref[pl.ds(half * 16 + g, R, stride=L * X), :] = tile


def exchange(rows):
    count = rows.shape[0]
    parts = lax.all_to_all(
        rows.reshape(B, count // B, Y), "sec", split_axis=0, concat_axis=0, tiled=True
    )
    return parts.reshape(count, Y)


def ring(count, place=lambda i: i, back=False):
    steps = [(place(i), place((i + 1) % count)) for i in range(count)]
    return [(target, source) for source, target in steps] if back else steps


def y_place(position):
    return position % B * 2 + position // B


def per_device(
    number, cotangent, growth_rate, section_factor, velocity, diffusivity, kernel, target
):
    send, own, factor, diff, kernel_in, target_in = call(
        pack_kernel,
        (
            shape(512, Y), shape(8, Y), shape(S, S), shape(S, S), shape(S, S),
            shape(S, S, dtype=jnp.int32),
        ),
        [hbm] * 8,
        "pack",
        scratch=(
            pltpu.VMEM((256, Y), f32),
            pltpu.VMEM((256, Y), f32),
            pltpu.VMEM((32, Y), f32),
            pltpu.VMEM((64, Y), f32),
            pltpu.VMEM((16, Y), f32),
            pltpu.SemaphoreType.DMA((8,)),
        ),
    )(
        number.reshape(256, Y),
        cotangent.reshape(256, Y),
        growth_rate.reshape(32, Y),
        velocity.reshape(64, Y),
        section_factor.reshape(1, S),
        diffusivity.reshape(1, S),
        kernel,
        target,
    )
    got = exchange(send)
    adj, coef, x_up, x_down, y_up, y_down = call(
        adjoint_kernel,
        (shape(256, Y), shape(COEF_ROWS, Y)) + (shape(EDGE_ROWS, Y),) * 4,
        [vmem] * 3,
        "adjoint",
    )(got, own, factor)
    x_count = lax.axis_size("gx")
    edges = (
        lax.ppermute(x_up, "gx", ring(x_count)),
        lax.ppermute(x_down, "gx", ring(x_count, back=True)),
        lax.ppermute(y_up, ("sec", "gy"), ring(2 * B, y_place)),
        lax.ppermute(y_down, ("sec", "gy"), ring(2 * B, y_place, True)),
    )
    gain, coag = call(
        pair_kernel,
        (shape(256, Y), shape(256, Y)),
        [vmem] * 4,
        "pairs",
        flops=1 << 32,
        nbytes=8 << 20,
        scratch=(
            pltpu.VMEM((S, 2 * Y), f32),
            pltpu.VMEM((S, 2 * Y), f32),
            pltpu.VMEM((S, 2 * Y), f32),
            pltpu.VMEM((2 * S * 8, Y), f32),
            pltpu.VMEM((WEIGHT_ROWS, 2 * S), bf16),
            pltpu.VMEM((6 * S, S), f32),
        ),
    )(got, adj, kernel_in, target_in)
    send_back = call(
        next_kernel, shape(512, Y), [vmem] * 11, "next", scratch=(pltpu.VMEM((256, Y), f32),)
    )(got, adj, own, diff, coef, gain, coag, *edges)
    next_rows, gradient = call(
        unpack_kernel, (shape(256, Y), shape(256, Y)), [vmem], "unpack"
    )(exchange(send_back))
    return next_rows.reshape(number.shape), gradient.reshape(number.shape)


def solution(mesh):
    return jax.shard_map(
        per_device,
        mesh=mesh,
        in_specs=(
            P("sec", None, "gx", "gy"),
            P("sec", None, "gx", "gy"),
            P(None, "gx", "gy"),
            P(),
            P(None, None, "gx", "gy"),
            P(),
            P(),
            P(),
        ),
        out_specs=(P("sec", None, "gx", "gy"), P("sec", None, "gx", "gy")),
        check_vma=False,
    )
```

time: 223 us -> 90.9 us (0.41)
  the two profiles are of different devices: /device:TPU:1 before, /device:TPU:32 now
where the time goes in v2:
time: 90.9 us; the launch traced here: 90.3 us
  blocking collectives  56.9 us (63%)
  Pallas kernels  13.6 us (15%)
  starting transfers between devices  13.5 us (15%)
  local copies, waits for them, and re-layouts  5.62 us (6%)
    all_to_all x2, blocking collectives, exchange(): lax.all_to_all(rows.reshape(B, count // B, Y), 'sec', split_axis=0, conca...  56.9 us
    pallas_call x1, Pallas kernels, per_device(): call(pair_kernel, (shape(256, Y), shape(256, Y)), [vmem] * 4, 'pairs', fl...  9.66 us
    ppermute x1, starting transfers between devices, per_device(): lax.ppermute(x_down, 'gx', ring(x_count, back=True))  5.75 us
    unnamed x16, local copies, waits for them, and re-layouts  5.62 us
    ppermute x1, starting transfers between devices, per_device(): lax.ppermute(y_up, ('sec', 'gy'), ring(2 * B, y_place))  3.62 us
    ppermute x1, starting transfers between devices, per_device(): lax.ppermute(y_down, ('sec', 'gy'), ring(2 * B, y_place, True))  2.22 us
    ppermute x1, starting transfers between devices, per_device(): lax.ppermute(x_up, 'gx', ring(x_count))  1.92 us
  transfers between devices with their start and end apart: 4, of which 0 were waited for; matrix products, arithmetic and copies ran while one was open for 0% of the time, Pallas kernels for 11%

profile of v2, /device:TPU:32, one launch (start us, length us, event | category | flops | bytes accessed | tf_op | source)
XLA Modules:
  0.0 90.3 jit_solution(10226389911828060960)
XLA Ops:
  0.6 0.0 copy-start.6
  0.6 0.0 copy-start.7
  0.7 0.6 copy-done.6
  1.3 0.0 copy-done.7
  1.3 0.0 copy-start
  1.3 0.9 copy-done
  2.2 0.0 copy-start.1
  2.2 0.9 copy-done.1
  3.1 0.0 copy-start.2
  3.1 0.8 copy-done.2
  4.0 0.0 copy-start.3
  4.0 0.8 copy-done.3
  4.8 0.0 copy-start.4
  4.8 0.8 copy-done.4
  5.6 0.0 copy-start.5
  5.6 0.7 copy-done.5
  6.3 1.5 %pack.1 = (f32[512,128]{1,0:T(8,128)S(1)}, f32[8,128]{1,0:T(8,128)S(1)}, f32[128,128]{1,0:T(8,128)S(1)}, f32[128,128]{1,0:T(8,128)S(1)}, f32[128,128]{1,0:T(8,128)S(1)}, /*index=5*/s32[128,128]{1,0:T(8,128)S(1)}) custom-call(f32[256,128]{1,0:T(8,128)S(1)} %bitcast.18, f32[256,128]{1,0:T(8,128)S(1)} %bitcast.19, f32[32,128]{1,0:T(8,128)S(1)} %bitcast.21, ...), custom_call_target="tpu_custom_call" | custom-call | bytes 1048576 | tf_op jit(solution)/shard_map/pack/pallas_call | solution.py:381
  7.8 32.9 %all_to_all.10 = f32[16,32,128]{2,1,0:T(8,128)S(1)} all-to-all(f32[16,32,128]{2,1,0:T(8,128)S(1)} %bitcast.17), channel_id=1, replica_groups=mesh['sec'=16,'gx'=16,'gy'=2] {'sec'}, dimensions={0} | all-to-all | bytes 524288 | tf_op jit(solution)/shard_map/all_to_all | solution.py:363
  40.7 0.5 adjoint.1
  41.2 1.9 %collective-permute-start = (f32[136,128]{1,0:T(8,128)S(1)}, f32[136,128]{1,0:T(8,128)S(1)}, u32[]{:S(2)}, u32[]{:S(2)}) collective-permute-start(f32[136,128]{1,0:T(8,128)S(1)} %get-tuple-element.28), channel_id=1, source_target_pairs={{0,2},{2,4},{4,6},{6,8},{8,10},{10,12},{12,14},{14,16},{16,18},{18... | collective-permute-start | bytes 208904 | tf_op jit(solution)/shard_map/ppermute | solution.py:416
  43.1 5.8 %collective-permute-start.1 = (f32[136,128]{1,0:T(8,128)S(1)}, f32[136,128]{1,0:T(8,128)S(1)}, u32[]{:S(2)}, u32[]{:S(2)}) collective-permute-start(f32[136,128]{1,0:T(8,128)S(1)} %get-tuple-element.29), channel_id=1, source_target_pairs={{2,0},{4,2},{6,4},{8,6},{10,8},{12,10},{14,12},{16,14},{18,16},{20... | collective-permute-start | bytes 208904 | tf_op jit(solution)/shard_map/ppermute | solution.py:417
  48.9 3.6 %collective-permute-start.2 = (f32[136,128]{1,0:T(8,128)S(1)}, f32[136,128]{1,0:T(8,128)S(1)}, u32[]{:S(2)}, u32[]{:S(2)}) collective-permute-start(f32[136,128]{1,0:T(8,128)S(1)} %get-tuple-element.30), channel_id=1, source_target_pairs={{0,32},{32,64},{64,96},{96,128},{128,160},{160,192},{192,224},{224... | collective-permute-start | bytes 208904 | tf_op jit(solution)/shard_map/ppermute | solution.py:418
  52.5 2.2 %collective-permute-start.3 = (f32[136,128]{1,0:T(8,128)S(1)}, f32[136,128]{1,0:T(8,128)S(1)}, u32[]{:S(2)}, u32[]{:S(2)}) collective-permute-start(f32[136,128]{1,0:T(8,128)S(1)} %get-tuple-element.31), channel_id=1, source_target_pairs={{32,0},{64,32},{96,64},{128,96},{160,128},{192,160},{224,192},{256... | collective-permute-start | bytes 208904 | tf_op jit(solution)/shard_map/ppermute | solution.py:419
  54.8 9.7 %pairs.1 = (f32[256,128]{1,0:T(8,128)S(1)}, f32[256,128]{1,0:T(8,128)S(1)}) custom-call(f32[512,128]{1,0:T(8,128)S(1)} %bitcast.13, f32[256,128]{1,0:T(8,128)S(1)} %get-tuple-element.21.adj_ref, f32[128,128]{1,0:T(8,128)S(1)} %get-tuple-element.24.kernel_ref, s32[128,128]{1,0:T(8,128)S(1)} %get-tuple-element.25.target_ref), custom_call_target="tpu_custom_call" | custom-call | flops 4294967296 | bytes 8388608 | tf_op jit(solution)/shard_map/pairs/pallas_call | solution.py:421
  64.4 0.0 collective-permute-done.low_x_ref
  64.4 0.0 collective-permute-done.1.high_x_ref
  64.4 0.0 collective-permute-done.2.low_y_ref
  64.5 0.0 collective-permute-done.3.high_y_ref
  64.5 0.7 next.1
  65.2 24.0 %all_to_all.11 = f32[16,32,128]{2,1,0:T(8,128)S(1)} all-to-all(f32[16,32,128]{2,1,0:T(8,128)S(1)} %bitcast.16), channel_id=1, replica_groups=mesh['sec'=16,'gx'=16,'gy'=2] {'sec'}, dimensions={0} | all-to-all | bytes 524288 | tf_op jit(solution)/shard_map/all_to_all | solution.py:363
  89.2 1.2 %unpack.1 = (f32[256,128]{1,0:T(8,128)}, f32[256,128]{1,0:T(8,128)}) custom-call(f32[512,128]{1,0:T(8,128)S(1)} %bitcast.15), custom_call_target="tpu_custom_call" | custom-call | bytes 1048576 | tf_op jit(solution)/shard_map/unpack/pallas_call | solution.py:440
Async XLA Ops:
  0.6 0.7 copy-start.6
  0.6 0.7 copy-start.7
  1.3 0.9 %copy-start = (f32[8,4,8,128]{3,2,1,0:T(8,128)S(1)}, f32[8,4,8,128]{3,2,1,0:T(8,128)}, u32[]{:S(2)}) copy-start(f32[8,4,8,128]{3,2,1,0:T(8,128)} %param.8) | copy-start | bytes 393220
  2.2 0.9 %copy-start.1 = (f32[8,4,8,128]{3,2,1,0:T(8,128)S(1)}, f32[8,4,8,128]{3,2,1,0:T(8,128)}, u32[]{:S(2)}) copy-start(f32[8,4,8,128]{3,2,1,0:T(8,128)} %param.9) | copy-start | bytes 393220
  3.1 0.8 copy-start.2
  4.0 0.8 copy-start.3
  4.8 0.8 copy-start.4
  5.6 0.7 copy-start.5
  41.2 23.2 %collective-permute-start = (f32[136,128]{1,0:T(8,128)S(1)}, f32[136,128]{1,0:T(8,128)S(1)}, u32[]{:S(2)}, u32[]{:S(2)}) collective-permute-start(f32[136,128]{1,0:T(8,128)S(1)} %get-tuple-element.28), channel_id=1, source_target_pairs={{0,2},{2,4},{4,6},{6,8},{8,10},{10,12},{12,14},{14,16},{16,18},{18... | collective-permute-start | bytes 208904 | tf_op jit(solution)/shard_map/ppermute | solution.py:416
  43.1 21.3 %collective-permute-start.1 = (f32[136,128]{1,0:T(8,128)S(1)}, f32[136,128]{1,0:T(8,128)S(1)}, u32[]{:S(2)}, u32[]{:S(2)}) collective-permute-start(f32[136,128]{1,0:T(8,128)S(1)} %get-tuple-element.29), channel_id=1, source_target_pairs={{2,0},{4,2},{6,4},{8,6},{10,8},{12,10},{14,12},{16,14},{18,16},{20... | collective-permute-start | bytes 208904 | tf_op jit(solution)/shard_map/ppermute | solution.py:417
  48.9 15.5 %collective-permute-start.2 = (f32[136,128]{1,0:T(8,128)S(1)}, f32[136,128]{1,0:T(8,128)S(1)}, u32[]{:S(2)}, u32[]{:S(2)}) collective-permute-start(f32[136,128]{1,0:T(8,128)S(1)} %get-tuple-element.30), channel_id=1, source_target_pairs={{0,32},{32,64},{64,96},{96,128},{128,160},{160,192},{192,224},{224... | collective-permute-start | bytes 208904 | tf_op jit(solution)/shard_map/ppermute | solution.py:418
  52.5 11.9 %collective-permute-start.3 = (f32[136,128]{1,0:T(8,128)S(1)}, f32[136,128]{1,0:T(8,128)S(1)}, u32[]{:S(2)}, u32[]{:S(2)}) collective-permute-start(f32[136,128]{1,0:T(8,128)S(1)} %get-tuple-element.31), channel_id=1, source_target_pairs={{32,0},{64,32},{96,64},{128,96},{160,128},{192,160},{224,192},{256... | collective-permute-start | bytes 208904 | tf_op jit(solution)/shard_map/ppermute | solution.py:419

commit v3 on v2

--- a/solution.py
+++ b/solution.py
@@ -18,7 +18,6 @@
 X = 8
 Y = 128
 GROUP = 16
-PER = 4
 
 INV, FWD, FWD_PI = (256 * i for i in range(3))
 FWD_Q = 768
@@ -71,8 +70,12 @@
     return tiles
 
 
-def own_cells(rows, device):
-    shift = lax.rem(Y - 8 * device, Y)
+def run_of(index):
+    return jnp.where(lax.axis_index("gy") == 0, index, B - 1 - index)
+
+
+def own_cells(rows, run):
+    shift = lax.rem(Y - 8 * run, Y)
     moved = pltpu.roll(pltpu.roll(rows, shift, 1), 0, 1, stride=8, stride_axis=0)
     group = lax.broadcasted_iota(jnp.int32, (B, Y), 1) // 8
     row = lax.broadcasted_iota(jnp.int32, (B, Y), 0)
@@ -84,7 +87,7 @@
     send_ref, own_ref, factor_ref, diff_ref, kernel_ref, target_ref,
     n_ref, c_ref, rate_ref, vel_ref, row_ref, sems,
 ):
-    device = lax.axis_index("sec")
+    run = run_of(lax.axis_index("sec"))
     pairs = (
         (n_hbm, n_ref),
         (c_hbm, c_ref),
@@ -105,11 +108,12 @@
                 ref[pl.ds(half * 16 + g, R, stride=L * X), :] for g in range(B)
             )
             for d, tile in enumerate(tiles):
-                send_ref[pl.ds(d * 32 + array * 16 + half * 8, 8), :] = tile
+                at = pl.multiple_of(run_of(d) * 32 + array * 16 + half * 8, 8)
+                send_ref[pl.ds(at, 8), :] = tile
     for copy in copies[2:]:
         copy.wait()
-    rows = [own_cells(rate_ref[pl.ds(h * 16, 16), :], device) for h in range(2)]
-    rows += [own_cells(vel_ref[pl.ds(h * 16, 16), :], device) for h in range(4)]
+    rows = [own_cells(rate_ref[pl.ds(h * 16, 16), :], run) for h in range(2)]
+    rows += [own_cells(vel_ref[pl.ds(h * 16, 16), :], run) for h in range(4)]
     own_ref[...] = jnp.concatenate(rows + [jnp.zeros((2, Y), f32)], axis=0)
     factor_ref[...] = jnp.broadcast_to(row_ref[pl.ds(0, 1), :], (S, S)).T
     diff_ref[...] = jnp.broadcast_to(row_ref[pl.ds(8, 1), :], (S, S)).T
@@ -125,7 +129,11 @@
     return tile if shift == 0 else pltpu.roll(tile, shift, 1)
 
 
-def pack_edges(tiles, which, refs, rows):
+def even_places():
+    return lax.rem(lax.axis_index("gx"), 2) == 0, lax.rem(run_of(lax.axis_index("sec")), 2) == 0
+
+
+def pack_edges(tiles, which, even, refs, rows):
     _, x, y = which
     x_up, x_down, y_up, y_down = (jnp.zeros((8, Y), f32) for _ in range(4))
     for i, tile in enumerate(tiles):
@@ -133,8 +141,17 @@
         x_down = jnp.where(x == 7 - i, turn(tile, 8 * (7 - i)), x_down)
         y_up = jnp.where(y == i, turn(tile, i - 7), y_up)
         y_down = jnp.where(y == 7 - i, turn(tile, 7 - i), y_down)
-    for ref, edge in zip(refs, (x_up, x_down, y_up, y_down)):
-        ref[rows, :] = edge
+    for i, (up, down) in enumerate(((x_up, x_down), (y_up, y_down))):
+        refs[2 * i][rows, :] = jnp.where(even[i], up, down)
+        refs[2 * i + 1][rows, :] = jnp.where(even[i], down, up)
+
+
+def received_edges(even, refs, rows):
+    edges = []
+    for i in range(2):
+        a, b = (ref[rows, :] for ref in refs[2 * i : 2 * i + 2])
+        edges += [jnp.where(even[i], b, a), jnp.where(even[i], a, b)]
+    return edges
 
 
 def shifted(tile, edges, i, which):
@@ -157,7 +174,7 @@
 
 
 def adjoint_kernel(
-    got_ref, own_ref, factor_ref, adj_ref, coef_ref, x_up_ref, x_down_ref, y_up_ref, y_down_ref
+    got_ref, own_ref, factor_ref, adj_ref, coef_ref, x_first_ref, x_second_ref, y_first_ref, y_second_ref
 ):
     block = lax.broadcasted_iota(jnp.int32, (B, Y), 0)
     for h in range(2):
@@ -195,13 +212,14 @@
         for i, local, product in values:
             adj_ref[pl.ds(h * S + i, B, stride=R), :] = local + product * carry
     which = lane_parts()
-    refs = (x_up_ref, x_down_ref, y_up_ref, y_down_ref)
+    even = even_places()
+    refs = (x_first_ref, x_second_ref, y_first_ref, y_second_ref)
     for b in range(B):
         tiles = [got_ref[pl.ds(b * 32 + h * 8, 8), :] for h in range(2)]
         tiles += [adj_ref[pl.ds(h * S + b * 8, 8), :] for h in range(2)]
-        pack_edges(tiles, which, refs, pl.ds(b * 8, 8))
+        pack_edges(tiles, which, even, refs, pl.ds(b * 8, 8))
     winds = [jnp.broadcast_to(own_ref[pl.ds(2 + h, 1), :], (8, Y)) for h in range(4)]
-    pack_edges(winds, which, refs, pl.ds(S, 8))
+    pack_edges(winds, which, even, refs, pl.ds(S, 8))
 
 
 def split(value):
@@ -241,7 +259,7 @@
             weight_ref[rows, :] = jnp.concatenate([high, rest], axis=1)
             return 0
 
-        lax.fori_loop(0, GROUP, build, 0)
+        lax.fori_loop(0, GROUP, build, 0, unroll=True)
 
     for r in range(2):
         for b in range(B):
@@ -256,24 +274,18 @@
         low = group * GROUP
         count = S - low
 
-        def visit(turns, _, low=low, count=count, start=OFFSETS[group]):
-            rows = pl.ds(pl.multiple_of(start + turns * (PER * count), 16), PER * count)
-            left = weight_ref[rows, :]
-            left = jnp.concatenate([left, left[:, :S]], axis=1)
-            found = jnp.dot(left, right, preferred_element_type=f32).reshape(PER, count, 2 * Y)
-            total = gain_ref[pl.ds(low, count), :]
-            adjoint = a_ref[pl.ds(low, count), :]
-            for p in range(PER):
-                k = low + turns * PER + p
-                total = total + found[p] * n_ref[pl.ds(k, 1), :]
-                share = (found[p] * adjoint).reshape(count // 8, 8, 2 * Y).sum(axis=0)
-                for r in range(2):
-                    rows = pl.ds(pl.multiple_of(r * 8 * S + k * 8, 8), 8)
-                    part_ref[rows, :] = share[:, r * Y : (r + 1) * Y]
-            gain_ref[pl.ds(low, count), :] = total
-            return 0
-
-        lax.fori_loop(0, GROUP // PER, visit, 0)
+        left = weight_ref[pl.ds(OFFSETS[group], GROUP * count), :]
+        left = jnp.concatenate([left, left[:, :S]], axis=1)
+        found = jnp.dot(left, right, preferred_element_type=f32).reshape(GROUP, count, 2 * Y)
+        total = gain_ref[pl.ds(low, count), :]
+        adjoint = a_ref[pl.ds(low, count), :]
+        for p in range(GROUP):
+            k = low + p
+            total = total + found[p] * n_ref[pl.ds(k, 1), :]
+            share = (found[p] * adjoint).reshape(count // 8, 8, 2 * Y).sum(axis=0)
+            for r in range(2):
+                part_ref[pl.ds(r * 8 * S + k * 8, 8), :] = share[:, r * Y : (r + 1) * Y]
+        gain_ref[pl.ds(low, count), :] = total
 
     adjoint = a_ref[...]
     pull = jnp.dot(kernel, number, precision=highest, preferred_element_type=f32)
@@ -291,11 +303,12 @@
 
 def next_kernel(
     got_ref, adj_ref, own_ref, diff_ref, coef_ref, gain_ref, coag_ref,
-    low_x_ref, high_x_ref, low_y_ref, high_y_ref, send_ref, right_ref,
+    x_first_ref, x_second_ref, y_first_ref, y_second_ref, send_ref, right_ref,
 ):
     which = lane_parts()
-    refs = (low_x_ref, high_x_ref, low_y_ref, high_y_ref)
-    wind_edges = [ref[pl.ds(S, 8), :] for ref in refs]
+    even = even_places()
+    refs = (x_first_ref, x_second_ref, y_first_ref, y_second_ref)
+    wind_edges = received_edges(even, refs, pl.ds(S, 8))
     winds = []
     for h in range(2):
         u = jnp.broadcast_to(own_ref[pl.ds(2 + h, 1), :], (8, Y))
@@ -304,7 +317,7 @@
         _, _, wp, wm = shifted(w, wind_edges, 2 + h, which)
         winds.append((0.5 * u, 0.5 * w, 0.5 * up, 0.5 * um, 0.5 * wp, 0.5 * wm))
     for b in range(B):
-        edges = [ref[pl.ds(b * 8, 8), :] for ref in refs]
+        edges = received_edges(even, refs, pl.ds(b * 8, 8))
         diffusion = diff_ref[pl.ds(b * 8, 8), :]
         numbers = [got_ref[pl.ds(b * 32 + h * 8, 8), :] for h in range(2)]
         adjoints = [adj_ref[pl.ds(h * S + b * 8, 8), :] for h in range(2)]
@@ -352,7 +365,8 @@
     for array, ref in enumerate((next_ref, gradient_ref)):
         for half in range(2):
             tiles = swap_groups(
-                back_ref[pl.ds(d * 32 + array * 16 + half * 8, 8), :] for d in range(B)
+                back_ref[pl.ds(pl.multiple_of(run_of(d) * 32 + array * 16 + half * 8, 8), 8), :]
+                for d in range(B)
             )
             for g, tile in enumerate(tiles):
                 ref[pl.ds(half * 16 + g, R, stride=L * X), :] = tile
@@ -366,13 +380,14 @@
     return parts.reshape(count, Y)
 
 
-def ring(count, place=lambda i: i, back=False):
-    steps = [(place(i), place((i + 1) % count)) for i in range(count)]
-    return [(target, source) for source, target in steps] if back else steps
+def swaps(count, first, place=lambda i: i):
+    pairs = [(place(i), place((i + 1) % count)) for i in range(first, count, 2)]
+    return pairs + [(b, a) for a, b in pairs]
 
 
 def y_place(position):
-    return position % B * 2 + position // B
+    half, run = position // B, position % B
+    return (B - 1 - run if half else run) * 2 + half
 
 
 def per_device(
@@ -395,17 +410,22 @@
             pltpu.SemaphoreType.DMA((8,)),
         ),
     )(
-        number.reshape(256, Y),
-        cotangent.reshape(256, Y),
-        growth_rate.reshape(32, Y),
-        velocity.reshape(64, Y),
-        section_factor.reshape(1, S),
-        diffusivity.reshape(1, S),
-        kernel,
-        target,
+        *(
+            pltpu.with_memory_space_constraint(array, pltpu.HBM)
+            for array in (
+                number.reshape(256, Y),
+                cotangent.reshape(256, Y),
+                growth_rate.reshape(32, Y),
+                velocity.reshape(64, Y),
+                section_factor.reshape(1, S),
+                diffusivity.reshape(1, S),
+                kernel,
+                target,
+            )
+        )
     )
     got = exchange(send)
-    adj, coef, x_up, x_down, y_up, y_down = call(
+    adj, coef, x_first, x_second, y_first, y_second = call(
         adjoint_kernel,
         (shape(256, Y), shape(COEF_ROWS, Y)) + (shape(EDGE_ROWS, Y),) * 4,
         [vmem] * 3,
@@ -413,10 +433,10 @@
     )(got, own, factor)
     x_count = lax.axis_size("gx")
     edges = (
-        lax.ppermute(x_up, "gx", ring(x_count)),
-        lax.ppermute(x_down, "gx", ring(x_count, back=True)),
-        lax.ppermute(y_up, ("sec", "gy"), ring(2 * B, y_place)),
-        lax.ppermute(y_down, ("sec", "gy"), ring(2 * B, y_place, True)),
+        lax.ppermute(x_first, "gx", swaps(x_count, 0)),
+        lax.ppermute(x_second, "gx", swaps(x_count, 1)),
+        lax.ppermute(y_first, ("sec", "gy"), swaps(2 * B, 0, y_place)),
+        lax.ppermute(y_second, ("sec", "gy"), swaps(2 * B, 1, y_place)),
     )
     gain, coag = call(
         pair_kernel,

time: 90.9 us -> 80 us (0.88)
  the two profiles are of different devices: /device:TPU:32 before, /device:TPU:40 now
where the time goes in v3:
time: 80 us; the launch traced here: 79.7 us
  blocking collectives  57.9 us (72%)
  starting transfers between devices  13.1 us (16%)
  Pallas kernels  7.99 us (10%)
    all_to_all x2, blocking collectives, exchange(): lax.all_to_all(rows.reshape(B, count // B, Y), 'sec', split_axis=0, conca...  57.9 us
    ppermute x1, starting transfers between devices, per_device(): lax.ppermute(x_second, 'gx', swaps(x_count, 1))  4.66 us
    ppermute x1, starting transfers between devices, per_device(): lax.ppermute(y_second, ('sec', 'gy'), swaps(2 * B, 1, y_place))  4.11 us
    pallas_call x1, Pallas kernels, per_device(): call(pair_kernel, (shape(256, Y), shape(256, Y)), [vmem] * 4, 'pairs', fl...  3.74 us
    ppermute x1, starting transfers between devices, per_device(): lax.ppermute(y_first, ('sec', 'gy'), swaps(2 * B, 0, y_place))  2.46 us
    ppermute x1, starting transfers between devices, per_device(): lax.ppermute(x_first, 'gx', swaps(x_count, 0))  1.92 us
    pallas_call x1, Pallas kernels, per_device(): call(pack_kernel, (shape(512, Y), shape(8, Y), shape(S, S), shape(S, S),...  1.9 us
  transfers between devices with their start and end apart: 4, of which 0 were waited for; matrix products, arithmetic and copies ran while one was open for 0% of the time, Pallas kernels for 5%

profile of v3, /device:TPU:40, one launch (start us, length us, event | category | flops | bytes accessed | tf_op | source)
XLA Modules:
  0.0 79.7 jit_solution(14494254326803124833)
XLA Ops:
  0.6 1.9 %pack.1 = (f32[512,128]{1,0:T(8,128)S(1)}, f32[8,128]{1,0:T(8,128)S(1)}, f32[128,128]{1,0:T(8,128)S(1)}, f32[128,128]{1,0:T(8,128)S(1)}, f32[128,128]{1,0:T(8,128)S(1)}, /*index=5*/s32[128,128]{1,0:T(8,128)S(1)}) custom-call(f32[256,128]{1,0:T(8,128)} %bitcast.18, f32[256,128]{1,0:T(8,128)} %bitcast.19, f32[32,128]{1,0:T(8,128)} %bitcast.21, ...), custom_call_target="tpu_custom_call" | custom-call | bytes 1048576 | tf_op jit(solution)/shard_map/pack/pallas_call | solution.py:396
  2.5 32.9 %all_to_all.10 = f32[16,32,128]{2,1,0:T(8,128)S(1)} all-to-all(f32[16,32,128]{2,1,0:T(8,128)S(1)} %bitcast.17), channel_id=1, replica_groups=mesh['sec'=16,'gx'=16,'gy'=2] {'sec'}, dimensions={0} | all-to-all | bytes 524288 | tf_op jit(solution)/shard_map/all_to_all | solution.py:377
  35.5 0.5 adjoint.1
  35.9 1.9 %collective-permute-start = (f32[136,128]{1,0:T(8,128)S(1)}, f32[136,128]{1,0:T(8,128)S(1)}, u32[]{:S(2)}, u32[]{:S(2)}) collective-permute-start(f32[136,128]{1,0:T(8,128)S(1)} %get-tuple-element.28), channel_id=1, source_target_pairs={{0,2},{4,6},{8,10},{12,14},{16,18},{20,22},{24,26},{28,30},{2,0},{... | collective-permute-start | bytes 208904 | tf_op jit(solution)/shard_map/ppermute | solution.py:436
  37.9 4.7 %collective-permute-start.1 = (f32[136,128]{1,0:T(8,128)S(1)}, f32[136,128]{1,0:T(8,128)S(1)}, u32[]{:S(2)}, u32[]{:S(2)}) collective-permute-start(f32[136,128]{1,0:T(8,128)S(1)} %get-tuple-element.29), channel_id=1, source_target_pairs={{2,4},{6,8},{10,12},{14,16},{18,20},{22,24},{26,28},{30,0},{4,2},{... | collective-permute-start | bytes 208904 | tf_op jit(solution)/shard_map/ppermute | solution.py:437
  42.5 2.5 %collective-permute-start.2 = (f32[136,128]{1,0:T(8,128)S(1)}, f32[136,128]{1,0:T(8,128)S(1)}, u32[]{:S(2)}, u32[]{:S(2)}) collective-permute-start(f32[136,128]{1,0:T(8,128)S(1)} %get-tuple-element.30), channel_id=1, source_target_pairs={{0,32},{64,96},{128,160},{192,224},{256,288},{320,352},{384,416},{... | collective-permute-start | bytes 208904 | tf_op jit(solution)/shard_map/ppermute | solution.py:438
  45.0 4.1 %collective-permute-start.3 = (f32[136,128]{1,0:T(8,128)S(1)}, f32[136,128]{1,0:T(8,128)S(1)}, u32[]{:S(2)}, u32[]{:S(2)}) collective-permute-start(f32[136,128]{1,0:T(8,128)S(1)} %get-tuple-element.31), channel_id=1, source_target_pairs={{32,64},{96,128},{160,192},{224,256},{288,320},{352,384},{416,448}... | collective-permute-start | bytes 208904 | tf_op jit(solution)/shard_map/ppermute | solution.py:439
  49.1 3.7 %pairs.1 = (f32[256,128]{1,0:T(8,128)S(1)}, f32[256,128]{1,0:T(8,128)S(1)}) custom-call(f32[512,128]{1,0:T(8,128)S(1)} %bitcast.13, f32[256,128]{1,0:T(8,128)S(1)} %get-tuple-element.21.adj_ref, f32[128,128]{1,0:T(8,128)S(1)} %get-tuple-element.24.kernel_ref, s32[128,128]{1,0:T(8,128)S(1)} %get-tuple-element.25.target_ref), custom_call_target="tpu_custom_call" | custom-call | flops 4294967296 | bytes 8388608 | tf_op jit(solution)/shard_map/pairs/pallas_call | solution.py:441
  52.9 0.0 collective-permute-done.x_first_ref
  52.9 0.0 collective-permute-done.1.x_second_ref
  52.9 0.0 collective-permute-done.2.y_first_ref
  52.9 0.0 collective-permute-done.3.y_second_ref
  52.9 0.7 next.1
  53.7 24.9 %all_to_all.11 = f32[16,32,128]{2,1,0:T(8,128)S(1)} all-to-all(f32[16,32,128]{2,1,0:T(8,128)S(1)} %bitcast.16), channel_id=1, replica_groups=mesh['sec'=16,'gx'=16,'gy'=2] {'sec'}, dimensions={0} | all-to-all | bytes 524288 | tf_op jit(solution)/shard_map/all_to_all | solution.py:377
  78.6 1.1 %unpack.1 = (f32[256,128]{1,0:T(8,128)}, f32[256,128]{1,0:T(8,128)}) custom-call(f32[512,128]{1,0:T(8,128)S(1)} %bitcast.15), custom_call_target="tpu_custom_call" | custom-call | bytes 1048576 | tf_op jit(solution)/shard_map/unpack/pallas_call | solution.py:460
Async XLA Ops:
  35.9 16.9 %collective-permute-start = (f32[136,128]{1,0:T(8,128)S(1)}, f32[136,128]{1,0:T(8,128)S(1)}, u32[]{:S(2)}, u32[]{:S(2)}) collective-permute-start(f32[136,128]{1,0:T(8,128)S(1)} %get-tuple-element.28), channel_id=1, source_target_pairs={{0,2},{4,6},{8,10},{12,14},{16,18},{20,22},{24,26},{28,30},{2,0},{... | collective-permute-start | bytes 208904 | tf_op jit(solution)/shard_map/ppermute | solution.py:436
  37.9 15.0 %collective-permute-start.1 = (f32[136,128]{1,0:T(8,128)S(1)}, f32[136,128]{1,0:T(8,128)S(1)}, u32[]{:S(2)}, u32[]{:S(2)}) collective-permute-start(f32[136,128]{1,0:T(8,128)S(1)} %get-tuple-element.29), channel_id=1, source_target_pairs={{2,4},{6,8},{10,12},{14,16},{18,20},{22,24},{26,28},{30,0},{4,2},{... | collective-permute-start | bytes 208904 | tf_op jit(solution)/shard_map/ppermute | solution.py:437
  42.5 10.4 %collective-permute-start.2 = (f32[136,128]{1,0:T(8,128)S(1)}, f32[136,128]{1,0:T(8,128)S(1)}, u32[]{:S(2)}, u32[]{:S(2)}) collective-permute-start(f32[136,128]{1,0:T(8,128)S(1)} %get-tuple-element.30), channel_id=1, source_target_pairs={{0,32},{64,96},{128,160},{192,224},{256,288},{320,352},{384,416},{... | collective-permute-start | bytes 208904 | tf_op jit(solution)/shard_map/ppermute | solution.py:438
  45.0 7.9 %collective-permute-start.3 = (f32[136,128]{1,0:T(8,128)S(1)}, f32[136,128]{1,0:T(8,128)S(1)}, u32[]{:S(2)}, u32[]{:S(2)}) collective-permute-start(f32[136,128]{1,0:T(8,128)S(1)} %get-tuple-element.31), channel_id=1, source_target_pairs={{32,64},{96,128},{160,192},{224,256},{288,320},{352,384},{416,448}... | collective-permute-start | bytes 208904 | tf_op jit(solution)/shard_map/ppermute | solution.py:439

commit v4 on v3

--- a/solution.py
+++ b/solution.py
@@ -39,17 +39,17 @@
 OFFSETS, WEIGHT_ROWS = row_offsets()
 
 
-def call(kernel, outs, in_specs, name, flops=0, nbytes=1 << 20, scratch=(), limit=None):
+def call(kernel, outs, in_specs, name, flops=0, nbytes=1 << 20, scratch=(), place=vmem):
     single = not isinstance(outs, (tuple, list))
     return pl.pallas_call(
         kernel,
         out_shape=outs,
         in_specs=in_specs,
-        out_specs=vmem if single else [vmem] * len(outs),
+        out_specs=place if single else [place] * len(outs),
         scratch_shapes=list(scratch),
         name=name,
         cost_estimate=pl.CostEstimate(flops=flops, bytes_accessed=nbytes, transcendentals=0),
-        compiler_params=pltpu.CompilerParams(vmem_limit_bytes=limit or (32 << 20)),
+        compiler_params=pltpu.CompilerParams(vmem_limit_bytes=32 << 20),
     )
 
 
@@ -60,14 +60,12 @@
 def swap_groups(tiles):
     group = lax.broadcasted_iota(jnp.int32, (8, Y), 1) // 8
     tiles = list(tiles)
+    tiles = [tiles[-i % B] for i in range(B)]
+    tiles = [pltpu.roll(tile, 8 * (-i % B), 1) if i else tile for i, tile in enumerate(tiles)]
     for bit in (1, 2, 4, 8):
         upper = (group & bit) != 0
-        for i in range(B):
-            if i & bit == 0:
-                a, b = tiles[i], tiles[i | bit]
-                tiles[i] = jnp.where(upper, pltpu.roll(b, 8 * bit, 1), a)
-                tiles[i | bit] = jnp.where(upper, b, pltpu.roll(a, Y - 8 * bit, 1))
-    return tiles
+        tiles = [jnp.where(upper, tiles[i - bit], tiles[i]) for i in range(B)]
+    return [pltpu.roll(tile, Y - 8 * i, 1) if i else tile for i, tile in enumerate(tiles)]
 
 
 def run_of(index):
@@ -89,20 +87,27 @@
 ):
     run = run_of(lax.axis_index("sec"))
     pairs = (
+        (factor_hbm, row_ref.at[pl.ds(0, 1)]),
+        (diff_hbm, row_ref.at[pl.ds(8, 1)]),
+        (rate_hbm, rate_ref),
+        (vel_hbm, vel_ref),
         (n_hbm, n_ref),
         (c_hbm, c_ref),
-        (rate_hbm, rate_ref),
-        (vel_hbm, vel_ref),
-        (factor_hbm, row_ref.at[pl.ds(0, 1)]),
-        (diff_hbm, row_ref.at[pl.ds(8, 1)]),
         (kernel_hbm, kernel_ref),
         (target_hbm, target_ref),
     )
     copies = [pltpu.make_async_copy(a, b, sems.at[i]) for i, (a, b) in enumerate(pairs)]
     for copy in copies:
         copy.start()
+    for copy in copies[:4]:
+        copy.wait()
+    rows = [own_cells(rate_ref[pl.ds(h * 16, 16), :], run) for h in range(2)]
+    rows += [own_cells(vel_ref[pl.ds(h * 16, 16), :], run) for h in range(4)]
+    own_ref[...] = jnp.concatenate(rows + [jnp.zeros((2, Y), f32)], axis=0)
+    factor_ref[...] = jnp.broadcast_to(row_ref[pl.ds(0, 1), :], (S, S)).T
+    diff_ref[...] = jnp.broadcast_to(row_ref[pl.ds(8, 1), :], (S, S)).T
     for array, ref in enumerate((n_ref, c_ref)):
-        copies[array].wait()
+        copies[4 + array].wait()
         for half in range(2):
             tiles = swap_groups(
                 ref[pl.ds(half * 16 + g, R, stride=L * X), :] for g in range(B)
@@ -110,13 +115,8 @@
             for d, tile in enumerate(tiles):
                 at = pl.multiple_of(run_of(d) * 32 + array * 16 + half * 8, 8)
                 send_ref[pl.ds(at, 8), :] = tile
-    for copy in copies[2:]:
+    for copy in copies[6:]:
         copy.wait()
-    rows = [own_cells(rate_ref[pl.ds(h * 16, 16), :], run) for h in range(2)]
-    rows += [own_cells(vel_ref[pl.ds(h * 16, 16), :], run) for h in range(4)]
-    own_ref[...] = jnp.concatenate(rows + [jnp.zeros((2, Y), f32)], axis=0)
-    factor_ref[...] = jnp.broadcast_to(row_ref[pl.ds(0, 1), :], (S, S)).T
-    diff_ref[...] = jnp.broadcast_to(row_ref[pl.ds(8, 1), :], (S, S)).T
 
 
 def lane_parts():
@@ -361,8 +361,9 @@
             send_ref[pl.ds(h * 8 + i, B, stride=32), :] = full
 
 
-def unpack_kernel(back_ref, next_ref, gradient_ref):
-    for array, ref in enumerate((next_ref, gradient_ref)):
+def unpack_kernel(back_ref, next_hbm, gradient_hbm, next_ref, gradient_ref, sems):
+    copies = []
+    for array, (ref, out) in enumerate(((next_ref, next_hbm), (gradient_ref, gradient_hbm))):
         for half in range(2):
             tiles = swap_groups(
                 back_ref[pl.ds(pl.multiple_of(run_of(d) * 32 + array * 16 + half * 8, 8), 8), :]
@@ -370,6 +371,10 @@
             )
             for g, tile in enumerate(tiles):
                 ref[pl.ds(half * 16 + g, R, stride=L * X), :] = tile
+        copies.append(pltpu.make_async_copy(ref, out, sems.at[array]))
+        copies[-1].start()
+    for copy in copies:
+        copy.wait()
 
 
 def exchange(rows):
@@ -458,7 +463,16 @@
         next_kernel, shape(512, Y), [vmem] * 11, "next", scratch=(pltpu.VMEM((256, Y), f32),)
     )(got, adj, own, diff, coef, gain, coag, *edges)
     next_rows, gradient = call(
-        unpack_kernel, (shape(256, Y), shape(256, Y)), [vmem], "unpack"
+        unpack_kernel,
+        (shape(256, Y), shape(256, Y)),
+        [vmem],
+        "unpack",
+        scratch=(
+            pltpu.VMEM((256, Y), f32),
+            pltpu.VMEM((256, Y), f32),
+            pltpu.SemaphoreType.DMA((2,)),
+        ),
+        place=hbm,
     )(exchange(send_back))
     return next_rows.reshape(number.shape), gradient.reshape(number.shape)
 

time: 80 us -> 79.5 us (level)
  no operation moved by 1% of the time
where the time goes in v4:
time: 79.5 us; the launch traced here: 79.2 us
  blocking collectives  57.9 us (73%)
  starting transfers between devices  13.1 us (16%)
  Pallas kernels  7.48 us (9%)
    all_to_all x2, blocking collectives, exchange(): lax.all_to_all(rows.reshape(B, count // B, Y), 'sec', split_axis=0, conca...  57.9 us
    ppermute x1, starting transfers between devices, per_device(): lax.ppermute(x_second, 'gx', swaps(x_count, 1))  4.66 us
    ppermute x1, starting transfers between devices, per_device(): lax.ppermute(y_second, ('sec', 'gy'), swaps(2 * B, 1, y_place))  4.11 us
    pallas_call x1, Pallas kernels, per_device(): call(pair_kernel, (shape(256, Y), shape(256, Y)), [vmem] * 4, 'pairs', fl...  3.74 us
    ppermute x1, starting transfers between devices, per_device(): lax.ppermute(y_first, ('sec', 'gy'), swaps(2 * B, 0, y_place))  2.46 us
    ppermute x1, starting transfers between devices, per_device(): lax.ppermute(x_first, 'gx', swaps(x_count, 0))  1.92 us
  transfers between devices with their start and end apart: 4, of which 0 were waited for; matrix products, arithmetic and copies ran while one was open for 0% of the time, Pallas kernels for 5%

profile of v4, /device:TPU:40, one launch (start us, length us, event | category | flops | bytes accessed | tf_op | source)
XLA Modules:
  0.0 79.2 jit_solution(2229510294106269654)
XLA Ops:
  0.6 1.6 %pack.1 = (f32[512,128]{1,0:T(8,128)S(1)}, f32[8,128]{1,0:T(8,128)S(1)}, f32[128,128]{1,0:T(8,128)S(1)}, f32[128,128]{1,0:T(8,128)S(1)}, f32[128,128]{1,0:T(8,128)S(1)}, /*index=5*/s32[128,128]{1,0:T(8,128)S(1)}) custom-call(f32[256,128]{1,0:T(8,128)} %bitcast.18, f32[256,128]{1,0:T(8,128)} %bitcast.19, f32[32,128]{1,0:T(8,128)} %bitcast.21, ...), custom_call_target="tpu_custom_call" | custom-call | bytes 1048576 | tf_op jit(solution)/shard_map/pack/pallas_call | solution.py:401
  2.2 32.9 %all_to_all.10 = f32[16,32,128]{2,1,0:T(8,128)S(1)} all-to-all(f32[16,32,128]{2,1,0:T(8,128)S(1)} %bitcast.17), channel_id=1, replica_groups=mesh['sec'=16,'gx'=16,'gy'=2] {'sec'}, dimensions={0} | all-to-all | bytes 524288 | tf_op jit(solution)/shard_map/all_to_all | solution.py:382
  35.1 0.5 adjoint.1
  35.6 1.9 %collective-permute-start = (f32[136,128]{1,0:T(8,128)S(1)}, f32[136,128]{1,0:T(8,128)S(1)}, u32[]{:S(2)}, u32[]{:S(2)}) collective-permute-start(f32[136,128]{1,0:T(8,128)S(1)} %get-tuple-element.28), channel_id=1, source_target_pairs={{0,2},{4,6},{8,10},{12,14},{16,18},{20,22},{24,26},{28,30},{2,0},{... | collective-permute-start | bytes 208904 | tf_op jit(solution)/shard_map/ppermute | solution.py:441
  37.5 4.7 %collective-permute-start.1 = (f32[136,128]{1,0:T(8,128)S(1)}, f32[136,128]{1,0:T(8,128)S(1)}, u32[]{:S(2)}, u32[]{:S(2)}) collective-permute-start(f32[136,128]{1,0:T(8,128)S(1)} %get-tuple-element.29), channel_id=1, source_target_pairs={{2,4},{6,8},{10,12},{14,16},{18,20},{22,24},{26,28},{30,0},{4,2},{... | collective-permute-start | bytes 208904 | tf_op jit(solution)/shard_map/ppermute | solution.py:442
  42.2 2.5 %collective-permute-start.2 = (f32[136,128]{1,0:T(8,128)S(1)}, f32[136,128]{1,0:T(8,128)S(1)}, u32[]{:S(2)}, u32[]{:S(2)}) collective-permute-start(f32[136,128]{1,0:T(8,128)S(1)} %get-tuple-element.30), channel_id=1, source_target_pairs={{0,32},{64,96},{128,160},{192,224},{256,288},{320,352},{384,416},{... | collective-permute-start | bytes 208904 | tf_op jit(solution)/shard_map/ppermute | solution.py:443
  44.7 4.1 %collective-permute-start.3 = (f32[136,128]{1,0:T(8,128)S(1)}, f32[136,128]{1,0:T(8,128)S(1)}, u32[]{:S(2)}, u32[]{:S(2)}) collective-permute-start(f32[136,128]{1,0:T(8,128)S(1)} %get-tuple-element.31), channel_id=1, source_target_pairs={{32,64},{96,128},{160,192},{224,256},{288,320},{352,384},{416,448}... | collective-permute-start | bytes 208904 | tf_op jit(solution)/shard_map/ppermute | solution.py:444
  48.8 3.7 %pairs.1 = (f32[256,128]{1,0:T(8,128)S(1)}, f32[256,128]{1,0:T(8,128)S(1)}) custom-call(f32[512,128]{1,0:T(8,128)S(1)} %bitcast.13, f32[256,128]{1,0:T(8,128)S(1)} %get-tuple-element.21.adj_ref, f32[128,128]{1,0:T(8,128)S(1)} %get-tuple-element.24.kernel_ref, s32[128,128]{1,0:T(8,128)S(1)} %get-tuple-element.25.target_ref), custom_call_target="tpu_custom_call" | custom-call | flops 4294967296 | bytes 8388608 | tf_op jit(solution)/shard_map/pairs/pallas_call | solution.py:446
  52.5 0.0 collective-permute-done.x_first_ref
  52.5 0.0 collective-permute-done.1.x_second_ref
  52.5 0.0 collective-permute-done.2.y_first_ref
  52.6 0.0 collective-permute-done.3.y_second_ref
  52.6 0.7 next.1
  53.3 25.0 %all_to_all.11 = f32[16,32,128]{2,1,0:T(8,128)S(1)} all-to-all(f32[16,32,128]{2,1,0:T(8,128)S(1)} %bitcast.16), channel_id=1, replica_groups=mesh['sec'=16,'gx'=16,'gy'=2] {'sec'}, dimensions={0} | all-to-all | bytes 524288 | tf_op jit(solution)/shard_map/all_to_all | solution.py:382
  78.3 1.0 %unpack.1 = (f32[256,128]{1,0:T(8,128)}, f32[256,128]{1,0:T(8,128)}) custom-call(f32[512,128]{1,0:T(8,128)S(1)} %bitcast.15), custom_call_target="tpu_custom_call" | custom-call | bytes 1048576 | tf_op jit(solution)/shard_map/unpack/pallas_call | solution.py:465
Async XLA Ops:
  35.6 16.9 %collective-permute-start = (f32[136,128]{1,0:T(8,128)S(1)}, f32[136,128]{1,0:T(8,128)S(1)}, u32[]{:S(2)}, u32[]{:S(2)}) collective-permute-start(f32[136,128]{1,0:T(8,128)S(1)} %get-tuple-element.28), channel_id=1, source_target_pairs={{0,2},{4,6},{8,10},{12,14},{16,18},{20,22},{24,26},{28,30},{2,0},{... | collective-permute-start | bytes 208904 | tf_op jit(solution)/shard_map/ppermute | solution.py:441
  37.5 15.0 %collective-permute-start.1 = (f32[136,128]{1,0:T(8,128)S(1)}, f32[136,128]{1,0:T(8,128)S(1)}, u32[]{:S(2)}, u32[]{:S(2)}) collective-permute-start(f32[136,128]{1,0:T(8,128)S(1)} %get-tuple-element.29), channel_id=1, source_target_pairs={{2,4},{6,8},{10,12},{14,16},{18,20},{22,24},{26,28},{30,0},{4,2},{... | collective-permute-start | bytes 208904 | tf_op jit(solution)/shard_map/ppermute | solution.py:442
  42.2 10.4 %collective-permute-start.2 = (f32[136,128]{1,0:T(8,128)S(1)}, f32[136,128]{1,0:T(8,128)S(1)}, u32[]{:S(2)}, u32[]{:S(2)}) collective-permute-start(f32[136,128]{1,0:T(8,128)S(1)} %get-tuple-element.30), channel_id=1, source_target_pairs={{0,32},{64,96},{128,160},{192,224},{256,288},{320,352},{384,416},{... | collective-permute-start | bytes 208904 | tf_op jit(solution)/shard_map/ppermute | solution.py:443
  44.7 7.9 %collective-permute-start.3 = (f32[136,128]{1,0:T(8,128)S(1)}, f32[136,128]{1,0:T(8,128)S(1)}, u32[]{:S(2)}, u32[]{:S(2)}) collective-permute-start(f32[136,128]{1,0:T(8,128)S(1)} %get-tuple-element.31), channel_id=1, source_target_pairs={{32,64},{96,128},{160,192},{224,256},{288,320},{352,384},{416,448}... | collective-permute-start | bytes 208904 | tf_op jit(solution)/shard_map/ppermute | solution.py:444

commit v5 on v4

--- a/solution.py
+++ b/solution.py
@@ -7,7 +7,6 @@
 
 step_size = 0.25
 vertical_mix = 0.2
-highest = lax.Precision.HIGHEST
 f32 = jnp.float32
 bf16 = jnp.bfloat16
 
@@ -227,6 +226,11 @@
     return high, (value - high.astype(f32)).astype(bf16)
 
 
+def three(value):
+    high, rest = split(value)
+    return jnp.concatenate([high, rest, high], axis=1)
+
+
 def pair_kernel(
     got_ref, adj_ref, kernel_ref, target_ref, gain_out, coag_out,
     n_ref, a_ref, gain_ref, part_ref, weight_ref, rows_ref,
@@ -238,11 +242,7 @@
     same = target == target_turned
     one = 0.5 * kernel + jnp.where(same, 0.5 * turned, 0.0)
     two = jnp.where(same, 0.0, 0.5 * turned)
-    one_high = one.astype(bf16).astype(f32)
-    two_high = two.astype(bf16).astype(f32)
-    for i, part in enumerate(
-        (target, target_turned, one_high, one - one_high, two_high, two - two_high)
-    ):
+    for i, part in enumerate((target, target_turned, one, two)):
         rows_ref[pl.ds(i * S, S), :] = part
 
     for group in range(S // GROUP):
@@ -251,10 +251,8 @@
         ids = (lax.broadcasted_iota(jnp.int32, (count, S), 0) + low).astype(f32)
 
         def build(k, _, low=low, count=count, ids=ids, start=OFFSETS[group]):
-            t1, t2, h1, l1, h2, l2 = (rows_ref[pl.ds(i * S + low + k, 1), :] for i in range(6))
-            hit1, hit2 = ids == t1, ids == t2
-            high = jnp.where(hit1, h1, jnp.where(hit2, h2, 0.0)).astype(bf16)
-            rest = jnp.where(hit1, l1, jnp.where(hit2, l2, 0.0)).astype(bf16)
+            t1, t2, one, two = (rows_ref[pl.ds(i * S + low + k, 1), :] for i in range(4))
+            high, rest = split(jnp.where(ids == t1, one, jnp.where(ids == t2, two, 0.0)))
             rows = pl.ds(pl.multiple_of(start + k * count, 16), count)
             weight_ref[rows, :] = jnp.concatenate([high, rest], axis=1)
             return 0
@@ -288,8 +286,10 @@
         gain_ref[pl.ds(low, count), :] = total
 
     adjoint = a_ref[...]
-    pull = jnp.dot(kernel, number, precision=highest, preferred_element_type=f32)
-    back = jnp.dot(turned, adjoint * number, precision=highest, preferred_element_type=f32)
+    pull = jnp.dot(three(kernel), right, preferred_element_type=f32)
+    high, rest = split(adjoint * number)
+    right = jnp.concatenate([high, high, rest], axis=0)
+    back = jnp.dot(three(turned), right, preferred_element_type=f32)
     gain = step_size * (0.5 * gain_ref[...] - number * pull)
     for r in range(2):
         gain_out[pl.ds(r * S, S), :] = gain[:, r * Y : (r + 1) * Y]
@@ -456,7 +456,7 @@
             pltpu.VMEM((S, 2 * Y), f32),
             pltpu.VMEM((2 * S * 8, Y), f32),
             pltpu.VMEM((WEIGHT_ROWS, 2 * S), bf16),
-            pltpu.VMEM((6 * S, S), f32),
+            pltpu.VMEM((4 * S, S), f32),
         ),
     )(got, adj, kernel_in, target_in)
     send_back = call(

time: 79.5 us -> 79.2 us (level)
  transfers between devices with their start and end apart: 4 -> 4, of which waited for: 0 -> 0; matrix products, arithmetic and copies ran while one was open for 0% -> 0% of each run, Pallas kernels for 5% -> 4%
where the time goes in v5:
time: 79.2 us; the launch traced here: 78.9 us
  blocking collectives  57.9 us (73%)
  starting transfers between devices  13.1 us (17%)
  Pallas kernels  7.17 us (9%)
    all_to_all x2, blocking collectives, exchange(): lax.all_to_all(rows.reshape(B, count // B, Y), 'sec', split_axis=0, conca...  57.9 us
    ppermute x1, starting transfers between devices, per_device(): lax.ppermute(x_second, 'gx', swaps(x_count, 1))  4.66 us
    ppermute x1, starting transfers between devices, per_device(): lax.ppermute(y_second, ('sec', 'gy'), swaps(2 * B, 1, y_place))  4.11 us
    pallas_call x1, Pallas kernels, per_device(): call(pair_kernel, (shape(256, Y), shape(256, Y)), [vmem] * 4, 'pairs', fl...  3.43 us
    ppermute x1, starting transfers between devices, per_device(): lax.ppermute(y_first, ('sec', 'gy'), swaps(2 * B, 0, y_place))  2.46 us
    ppermute x1, starting transfers between devices, per_device(): lax.ppermute(x_first, 'gx', swaps(x_count, 0))  1.92 us
  transfers between devices with their start and end apart: 4, of which 0 were waited for; matrix products, arithmetic and copies ran while one was open for 0% of the time, Pallas kernels for 4%

profile of v5, /device:TPU:40, one launch (start us, length us, event | category | flops | bytes accessed | tf_op | source)
XLA Modules:
  0.0 78.9 jit_solution(4332575854814361459)
XLA Ops:
  0.6 1.6 %pack.1 = (f32[512,128]{1,0:T(8,128)S(1)}, f32[8,128]{1,0:T(8,128)S(1)}, f32[128,128]{1,0:T(8,128)S(1)}, f32[128,128]{1,0:T(8,128)S(1)}, f32[128,128]{1,0:T(8,128)S(1)}, /*index=5*/s32[128,128]{1,0:T(8,128)S(1)}) custom-call(f32[256,128]{1,0:T(8,128)} %bitcast.18, f32[256,128]{1,0:T(8,128)} %bitcast.19, f32[32,128]{1,0:T(8,128)} %bitcast.21, ...), custom_call_target="tpu_custom_call" | custom-call | bytes 1048576 | tf_op jit(solution)/shard_map/pack/pallas_call | solution.py:401
  2.2 32.9 %all_to_all.10 = f32[16,32,128]{2,1,0:T(8,128)S(1)} all-to-all(f32[16,32,128]{2,1,0:T(8,128)S(1)} %bitcast.17), channel_id=1, replica_groups=mesh['sec'=16,'gx'=16,'gy'=2] {'sec'}, dimensions={0} | all-to-all | bytes 524288 | tf_op jit(solution)/shard_map/all_to_all | solution.py:382
  35.1 0.5 adjoint.1
  35.6 1.9 %collective-permute-start = (f32[136,128]{1,0:T(8,128)S(1)}, f32[136,128]{1,0:T(8,128)S(1)}, u32[]{:S(2)}, u32[]{:S(2)}) collective-permute-start(f32[136,128]{1,0:T(8,128)S(1)} %get-tuple-element.28), channel_id=1, source_target_pairs={{0,2},{4,6},{8,10},{12,14},{16,18},{20,22},{24,26},{28,30},{2,0},{... | collective-permute-start | bytes 208904 | tf_op jit(solution)/shard_map/ppermute | solution.py:441
  37.5 4.7 %collective-permute-start.1 = (f32[136,128]{1,0:T(8,128)S(1)}, f32[136,128]{1,0:T(8,128)S(1)}, u32[]{:S(2)}, u32[]{:S(2)}) collective-permute-start(f32[136,128]{1,0:T(8,128)S(1)} %get-tuple-element.29), channel_id=1, source_target_pairs={{2,4},{6,8},{10,12},{14,16},{18,20},{22,24},{26,28},{30,0},{4,2},{... | collective-permute-start | bytes 208904 | tf_op jit(solution)/shard_map/ppermute | solution.py:442
  42.2 2.5 %collective-permute-start.2 = (f32[136,128]{1,0:T(8,128)S(1)}, f32[136,128]{1,0:T(8,128)S(1)}, u32[]{:S(2)}, u32[]{:S(2)}) collective-permute-start(f32[136,128]{1,0:T(8,128)S(1)} %get-tuple-element.30), channel_id=1, source_target_pairs={{0,32},{64,96},{128,160},{192,224},{256,288},{320,352},{384,416},{... | collective-permute-start | bytes 208904 | tf_op jit(solution)/shard_map/ppermute | solution.py:443
  44.7 4.1 %collective-permute-start.3 = (f32[136,128]{1,0:T(8,128)S(1)}, f32[136,128]{1,0:T(8,128)S(1)}, u32[]{:S(2)}, u32[]{:S(2)}) collective-permute-start(f32[136,128]{1,0:T(8,128)S(1)} %get-tuple-element.31), channel_id=1, source_target_pairs={{32,64},{96,128},{160,192},{224,256},{288,320},{352,384},{416,448}... | collective-permute-start | bytes 208904 | tf_op jit(solution)/shard_map/ppermute | solution.py:444
  48.8 3.4 %pairs.1 = (f32[256,128]{1,0:T(8,128)S(1)}, f32[256,128]{1,0:T(8,128)S(1)}) custom-call(f32[512,128]{1,0:T(8,128)S(1)} %bitcast.13, f32[256,128]{1,0:T(8,128)S(1)} %get-tuple-element.21.adj_ref, f32[128,128]{1,0:T(8,128)S(1)} %get-tuple-element.24.kernel_ref, s32[128,128]{1,0:T(8,128)S(1)} %get-tuple-element.25.target_ref), custom_call_target="tpu_custom_call" | custom-call | flops 4294967296 | bytes 8388608 | tf_op jit(solution)/shard_map/pairs/pallas_call | solution.py:446
  52.2 0.0 collective-permute-done.x_first_ref
  52.2 0.0 collective-permute-done.1.x_second_ref
  52.2 0.0 collective-permute-done.2.y_first_ref
  52.2 0.0 collective-permute-done.3.y_second_ref
  52.2 0.7 next.1
  53.0 24.9 %all_to_all.11 = f32[16,32,128]{2,1,0:T(8,128)S(1)} all-to-all(f32[16,32,128]{2,1,0:T(8,128)S(1)} %bitcast.16), channel_id=1, replica_groups=mesh['sec'=16,'gx'=16,'gy'=2] {'sec'}, dimensions={0} | all-to-all | bytes 524288 | tf_op jit(solution)/shard_map/all_to_all | solution.py:382
  78.0 1.0 %unpack.1 = (f32[256,128]{1,0:T(8,128)}, f32[256,128]{1,0:T(8,128)}) custom-call(f32[512,128]{1,0:T(8,128)S(1)} %bitcast.15), custom_call_target="tpu_custom_call" | custom-call | bytes 1048576 | tf_op jit(solution)/shard_map/unpack/pallas_call | solution.py:465
Async XLA Ops:
  35.6 16.6 %collective-permute-start = (f32[136,128]{1,0:T(8,128)S(1)}, f32[136,128]{1,0:T(8,128)S(1)}, u32[]{:S(2)}, u32[]{:S(2)}) collective-permute-start(f32[136,128]{1,0:T(8,128)S(1)} %get-tuple-element.28), channel_id=1, source_target_pairs={{0,2},{4,6},{8,10},{12,14},{16,18},{20,22},{24,26},{28,30},{2,0},{... | collective-permute-start | bytes 208904 | tf_op jit(solution)/shard_map/ppermute | solution.py:441
  37.5 14.7 %collective-permute-start.1 = (f32[136,128]{1,0:T(8,128)S(1)}, f32[136,128]{1,0:T(8,128)S(1)}, u32[]{:S(2)}, u32[]{:S(2)}) collective-permute-start(f32[136,128]{1,0:T(8,128)S(1)} %get-tuple-element.29), channel_id=1, source_target_pairs={{2,4},{6,8},{10,12},{14,16},{18,20},{22,24},{26,28},{30,0},{4,2},{... | collective-permute-start | bytes 208904 | tf_op jit(solution)/shard_map/ppermute | solution.py:442
  42.2 10.0 %collective-permute-start.2 = (f32[136,128]{1,0:T(8,128)S(1)}, f32[136,128]{1,0:T(8,128)S(1)}, u32[]{:S(2)}, u32[]{:S(2)}) collective-permute-start(f32[136,128]{1,0:T(8,128)S(1)} %get-tuple-element.30), channel_id=1, source_target_pairs={{0,32},{64,96},{128,160},{192,224},{256,288},{320,352},{384,416},{... | collective-permute-start | bytes 208904 | tf_op jit(solution)/shard_map/ppermute | solution.py:443
  44.7 7.6 %collective-permute-start.3 = (f32[136,128]{1,0:T(8,128)S(1)}, f32[136,128]{1,0:T(8,128)S(1)}, u32[]{:S(2)}, u32[]{:S(2)}) collective-permute-start(f32[136,128]{1,0:T(8,128)S(1)} %get-tuple-element.31), channel_id=1, source_target_pairs={{32,64},{96,128},{160,192},{224,256},{288,320},{352,384},{416,448}... | collective-permute-start | bytes 208904 | tf_op jit(solution)/shard_map/ppermute | solution.py:444

commit v6 on v5

--- a/solution.py
+++ b/solution.py
@@ -7,6 +7,7 @@
 
 step_size = 0.25
 vertical_mix = 0.2
+highest = lax.Precision.HIGHEST
 f32 = jnp.float32
 bf16 = jnp.bfloat16
 
@@ -226,11 +227,6 @@
     return high, (value - high.astype(f32)).astype(bf16)
 
 
-def three(value):
-    high, rest = split(value)
-    return jnp.concatenate([high, rest, high], axis=1)
-
-
 def pair_kernel(
     got_ref, adj_ref, kernel_ref, target_ref, gain_out, coag_out,
     n_ref, a_ref, gain_ref, part_ref, weight_ref, rows_ref,
@@ -286,10 +282,8 @@
         gain_ref[pl.ds(low, count), :] = total
 
     adjoint = a_ref[...]
-    pull = jnp.dot(three(kernel), right, preferred_element_type=f32)
-    high, rest = split(adjoint * number)
-    right = jnp.concatenate([high, high, rest], axis=0)
-    back = jnp.dot(three(turned), right, preferred_element_type=f32)
+    pull = jnp.dot(kernel, number, precision=highest, preferred_element_type=f32)
+    back = jnp.dot(turned, adjoint * number, precision=highest, preferred_element_type=f32)
     gain = step_size * (0.5 * gain_ref[...] - number * pull)
     for r in range(2):
         gain_out[pl.ds(r * S, S), :] = gain[:, r * Y : (r + 1) * Y]

time: 79.2 us -> 79.3 us (level)
  transfers between devices with their start and end apart: 4 -> 4, of which waited for: 0 -> 0; matrix products, arithmetic and copies ran while one was open for 0% -> 0% of each run, Pallas kernels for 4% -> 5%
where the time goes in v6:
time: 79.3 us; the launch traced here: 79.1 us
  blocking collectives  57.9 us (73%)
  starting transfers between devices  13.1 us (17%)
  Pallas kernels  7.3 us (9%)
    all_to_all x2, blocking collectives, exchange(): lax.all_to_all(rows.reshape(B, count // B, Y), 'sec', split_axis=0, conca...  57.9 us
    ppermute x1, starting transfers between devices, per_device(): lax.ppermute(x_second, 'gx', swaps(x_count, 1))  4.66 us
    ppermute x1, starting transfers between devices, per_device(): lax.ppermute(y_second, ('sec', 'gy'), swaps(2 * B, 1, y_place))  4.11 us
    pallas_call x1, Pallas kernels, per_device(): call(pair_kernel, (shape(256, Y), shape(256, Y)), [vmem] * 4, 'pairs', fl...  3.56 us
    ppermute x1, starting transfers between devices, per_device(): lax.ppermute(y_first, ('sec', 'gy'), swaps(2 * B, 0, y_place))  2.46 us
    ppermute x1, starting transfers between devices, per_device(): lax.ppermute(x_first, 'gx', swaps(x_count, 0))  1.92 us
  transfers between devices with their start and end apart: 4, of which 0 were waited for; matrix products, arithmetic and copies ran while one was open for 0% of the time, Pallas kernels for 5%

profile of v6, /device:TPU:40, one launch (start us, length us, event | category | flops | bytes accessed | tf_op | source)
XLA Modules:
  0.0 79.1 jit_solution(9581971361443859374)
XLA Ops:
  0.6 1.6 %pack.1 = (f32[512,128]{1,0:T(8,128)S(1)}, f32[8,128]{1,0:T(8,128)S(1)}, f32[128,128]{1,0:T(8,128)S(1)}, f32[128,128]{1,0:T(8,128)S(1)}, f32[128,128]{1,0:T(8,128)S(1)}, /*index=5*/s32[128,128]{1,0:T(8,128)S(1)}) custom-call(f32[256,128]{1,0:T(8,128)} %bitcast.18, f32[256,128]{1,0:T(8,128)} %bitcast.19, f32[32,128]{1,0:T(8,128)} %bitcast.21, ...), custom_call_target="tpu_custom_call" | custom-call | bytes 1048576 | tf_op jit(solution)/shard_map/pack/pallas_call | solution.py:395
  2.2 32.9 %all_to_all.10 = f32[16,32,128]{2,1,0:T(8,128)S(1)} all-to-all(f32[16,32,128]{2,1,0:T(8,128)S(1)} %bitcast.17), channel_id=1, replica_groups=mesh['sec'=16,'gx'=16,'gy'=2] {'sec'}, dimensions={0} | all-to-all | bytes 524288 | tf_op jit(solution)/shard_map/all_to_all | solution.py:376
  35.1 0.5 adjoint.1
  35.6 1.9 %collective-permute-start = (f32[136,128]{1,0:T(8,128)S(1)}, f32[136,128]{1,0:T(8,128)S(1)}, u32[]{:S(2)}, u32[]{:S(2)}) collective-permute-start(f32[136,128]{1,0:T(8,128)S(1)} %get-tuple-element.28), channel_id=1, source_target_pairs={{0,2},{4,6},{8,10},{12,14},{16,18},{20,22},{24,26},{28,30},{2,0},{... | collective-permute-start | bytes 208904 | tf_op jit(solution)/shard_map/ppermute | solution.py:435
  37.5 4.7 %collective-permute-start.1 = (f32[136,128]{1,0:T(8,128)S(1)}, f32[136,128]{1,0:T(8,128)S(1)}, u32[]{:S(2)}, u32[]{:S(2)}) collective-permute-start(f32[136,128]{1,0:T(8,128)S(1)} %get-tuple-element.29), channel_id=1, source_target_pairs={{2,4},{6,8},{10,12},{14,16},{18,20},{22,24},{26,28},{30,0},{4,2},{... | collective-permute-start | bytes 208904 | tf_op jit(solution)/shard_map/ppermute | solution.py:436
  42.2 2.5 %collective-permute-start.2 = (f32[136,128]{1,0:T(8,128)S(1)}, f32[136,128]{1,0:T(8,128)S(1)}, u32[]{:S(2)}, u32[]{:S(2)}) collective-permute-start(f32[136,128]{1,0:T(8,128)S(1)} %get-tuple-element.30), channel_id=1, source_target_pairs={{0,32},{64,96},{128,160},{192,224},{256,288},{320,352},{384,416},{... | collective-permute-start | bytes 208904 | tf_op jit(solution)/shard_map/ppermute | solution.py:437
  44.7 4.1 %collective-permute-start.3 = (f32[136,128]{1,0:T(8,128)S(1)}, f32[136,128]{1,0:T(8,128)S(1)}, u32[]{:S(2)}, u32[]{:S(2)}) collective-permute-start(f32[136,128]{1,0:T(8,128)S(1)} %get-tuple-element.31), channel_id=1, source_target_pairs={{32,64},{96,128},{160,192},{224,256},{288,320},{352,384},{416,448}... | collective-permute-start | bytes 208904 | tf_op jit(solution)/shard_map/ppermute | solution.py:438
  48.8 3.6 %pairs.1 = (f32[256,128]{1,0:T(8,128)S(1)}, f32[256,128]{1,0:T(8,128)S(1)}) custom-call(f32[512,128]{1,0:T(8,128)S(1)} %bitcast.13, f32[256,128]{1,0:T(8,128)S(1)} %get-tuple-element.21.adj_ref, f32[128,128]{1,0:T(8,128)S(1)} %get-tuple-element.24.kernel_ref, s32[128,128]{1,0:T(8,128)S(1)} %get-tuple-element.25.target_ref), custom_call_target="tpu_custom_call" | custom-call | flops 4294967296 | bytes 8388608 | tf_op jit(solution)/shard_map/pairs/pallas_call | solution.py:440
  52.3 0.0 collective-permute-done.x_first_ref
  52.4 0.0 collective-permute-done.1.x_second_ref
  52.4 0.0 collective-permute-done.2.y_first_ref
  52.4 0.0 collective-permute-done.3.y_second_ref
  52.4 0.7 next.1
  53.1 25.0 %all_to_all.11 = f32[16,32,128]{2,1,0:T(8,128)S(1)} all-to-all(f32[16,32,128]{2,1,0:T(8,128)S(1)} %bitcast.16), channel_id=1, replica_groups=mesh['sec'=16,'gx'=16,'gy'=2] {'sec'}, dimensions={0} | all-to-all | bytes 524288 | tf_op jit(solution)/shard_map/all_to_all | solution.py:376
  78.1 1.0 %unpack.1 = (f32[256,128]{1,0:T(8,128)}, f32[256,128]{1,0:T(8,128)}) custom-call(f32[512,128]{1,0:T(8,128)S(1)} %bitcast.15), custom_call_target="tpu_custom_call" | custom-call | bytes 1048576 | tf_op jit(solution)/shard_map/unpack/pallas_call | solution.py:459
Async XLA Ops:
  35.6 16.8 %collective-permute-start = (f32[136,128]{1,0:T(8,128)S(1)}, f32[136,128]{1,0:T(8,128)S(1)}, u32[]{:S(2)}, u32[]{:S(2)}) collective-permute-start(f32[136,128]{1,0:T(8,128)S(1)} %get-tuple-element.28), channel_id=1, source_target_pairs={{0,2},{4,6},{8,10},{12,14},{16,18},{20,22},{24,26},{28,30},{2,0},{... | collective-permute-start | bytes 208904 | tf_op jit(solution)/shard_map/ppermute | solution.py:435
  37.5 14.8 %collective-permute-start.1 = (f32[136,128]{1,0:T(8,128)S(1)}, f32[136,128]{1,0:T(8,128)S(1)}, u32[]{:S(2)}, u32[]{:S(2)}) collective-permute-start(f32[136,128]{1,0:T(8,128)S(1)} %get-tuple-element.29), channel_id=1, source_target_pairs={{2,4},{6,8},{10,12},{14,16},{18,20},{22,24},{26,28},{30,0},{4,2},{... | collective-permute-start | bytes 208904 | tf_op jit(solution)/shard_map/ppermute | solution.py:436
  42.2 10.2 %collective-permute-start.2 = (f32[136,128]{1,0:T(8,128)S(1)}, f32[136,128]{1,0:T(8,128)S(1)}, u32[]{:S(2)}, u32[]{:S(2)}) collective-permute-start(f32[136,128]{1,0:T(8,128)S(1)} %get-tuple-element.30), channel_id=1, source_target_pairs={{0,32},{64,96},{128,160},{192,224},{256,288},{320,352},{384,416},{... | collective-permute-start | bytes 208904 | tf_op jit(solution)/shard_map/ppermute | solution.py:437
  44.7 7.7 %collective-permute-start.3 = (f32[136,128]{1,0:T(8,128)S(1)}, f32[136,128]{1,0:T(8,128)S(1)}, u32[]{:S(2)}, u32[]{:S(2)}) collective-permute-start(f32[136,128]{1,0:T(8,128)S(1)} %get-tuple-element.31), channel_id=1, source_target_pairs={{32,64},{96,128},{160,192},{224,256},{288,320},{352,384},{416,448}... | collective-permute-start | bytes 208904 | tf_op jit(solution)/shard_map/ppermute | solution.py:438

commit v7 on v6

--- a/solution.py
+++ b/solution.py
@@ -297,7 +297,7 @@
 
 def next_kernel(
     got_ref, adj_ref, own_ref, diff_ref, coef_ref, gain_ref, coag_ref,
-    x_first_ref, x_second_ref, y_first_ref, y_second_ref, send_ref, right_ref,
+    y_second_ref, y_first_ref, x_second_ref, x_first_ref, send_ref, right_ref,
 ):
     which = lane_parts()
     even = even_places()
@@ -455,7 +455,7 @@
     )(got, adj, kernel_in, target_in)
     send_back = call(
         next_kernel, shape(512, Y), [vmem] * 11, "next", scratch=(pltpu.VMEM((256, Y), f32),)
-    )(got, adj, own, diff, coef, gain, coag, *edges)
+    )(got, adj, own, diff, coef, gain, coag, *edges[::-1])
     next_rows, gradient = call(
         unpack_kernel,
         (shape(256, Y), shape(256, Y)),

time: 79.3 us -> 79.5 us (level)
  the two profiles are of different devices: /device:TPU:40 before, /device:TPU:32 now
where the time goes in v7:
time: 79.5 us; the launch traced here: 79.2 us
  blocking collectives  58.2 us (73%)
  starting transfers between devices  13 us (16%)
  Pallas kernels  7.3 us (9%)
    all_to_all x2, blocking collectives, exchange(): lax.all_to_all(rows.reshape(B, count // B, Y), 'sec', split_axis=0, conca...  58.2 us
    ppermute x1, starting transfers between devices, per_device(): lax.ppermute(y_first, ('sec', 'gy'), swaps(2 * B, 0, y_place))  3.94 us
    ppermute x1, starting transfers between devices, per_device(): lax.ppermute(y_second, ('sec', 'gy'), swaps(2 * B, 1, y_place))  3.62 us
    pallas_call x1, Pallas kernels, per_device(): call(pair_kernel, (shape(256, Y), shape(256, Y)), [vmem] * 4, 'pairs', fl...  3.56 us
    ppermute x1, starting transfers between devices, per_device(): lax.ppermute(x_first, 'gx', swaps(x_count, 0))  3.5 us
    ppermute x1, starting transfers between devices, per_device(): lax.ppermute(x_second, 'gx', swaps(x_count, 1))  1.92 us
  transfers between devices with their start and end apart: 4, of which 0 were waited for; matrix products, arithmetic and copies ran while one was open for 0% of the time, Pallas kernels for 4%

profile of v7, /device:TPU:32, one launch (start us, length us, event | category | flops | bytes accessed | tf_op | source)
XLA Modules:
  0.0 79.2 jit_solution(1789665936826679711)
XLA Ops:
  0.6 1.6 %pack.1 = (f32[512,128]{1,0:T(8,128)S(1)}, f32[8,128]{1,0:T(8,128)S(1)}, f32[128,128]{1,0:T(8,128)S(1)}, f32[128,128]{1,0:T(8,128)S(1)}, f32[128,128]{1,0:T(8,128)S(1)}, /*index=5*/s32[128,128]{1,0:T(8,128)S(1)}) custom-call(f32[256,128]{1,0:T(8,128)} %bitcast.18, f32[256,128]{1,0:T(8,128)} %bitcast.19, f32[32,128]{1,0:T(8,128)} %bitcast.21, ...), custom_call_target="tpu_custom_call" | custom-call | bytes 1048576 | tf_op jit(solution)/shard_map/pack/pallas_call | solution.py:395
  2.2 32.9 %all_to_all.10 = f32[16,32,128]{2,1,0:T(8,128)S(1)} all-to-all(f32[16,32,128]{2,1,0:T(8,128)S(1)} %bitcast.17), channel_id=1, replica_groups=mesh['sec'=16,'gx'=16,'gy'=2] {'sec'}, dimensions={0} | all-to-all | bytes 524288 | tf_op jit(solution)/shard_map/all_to_all | solution.py:376
  35.1 0.5 adjoint.1
  35.6 3.6 %collective-permute-start = (f32[136,128]{1,0:T(8,128)S(1)}, f32[136,128]{1,0:T(8,128)S(1)}, u32[]{:S(2)}, u32[]{:S(2)}) collective-permute-start(f32[136,128]{1,0:T(8,128)S(1)} %get-tuple-element.28), channel_id=1, source_target_pairs={{32,64},{96,128},{160,192},{224,256},{288,320},{352,384},{416,448}... | collective-permute-start | bytes 208904 | tf_op jit(solution)/shard_map/ppermute | solution.py:438
  39.2 3.9 %collective-permute-start.1 = (f32[136,128]{1,0:T(8,128)S(1)}, f32[136,128]{1,0:T(8,128)S(1)}, u32[]{:S(2)}, u32[]{:S(2)}) collective-permute-start(f32[136,128]{1,0:T(8,128)S(1)} %get-tuple-element.29), channel_id=1, source_target_pairs={{0,32},{64,96},{128,160},{192,224},{256,288},{320,352},{384,416},{... | collective-permute-start | bytes 208904 | tf_op jit(solution)/shard_map/ppermute | solution.py:437
  43.2 1.9 %collective-permute-start.2 = (f32[136,128]{1,0:T(8,128)S(1)}, f32[136,128]{1,0:T(8,128)S(1)}, u32[]{:S(2)}, u32[]{:S(2)}) collective-permute-start(f32[136,128]{1,0:T(8,128)S(1)} %get-tuple-element.30), channel_id=1, source_target_pairs={{2,4},{6,8},{10,12},{14,16},{18,20},{22,24},{26,28},{30,0},{4,2},{... | collective-permute-start | bytes 208904 | tf_op jit(solution)/shard_map/ppermute | solution.py:436
  45.1 3.5 %collective-permute-start.3 = (f32[136,128]{1,0:T(8,128)S(1)}, f32[136,128]{1,0:T(8,128)S(1)}, u32[]{:S(2)}, u32[]{:S(2)}) collective-permute-start(f32[136,128]{1,0:T(8,128)S(1)} %get-tuple-element.31), channel_id=1, source_target_pairs={{0,2},{4,6},{8,10},{12,14},{16,18},{20,22},{24,26},{28,30},{2,0},{... | collective-permute-start | bytes 208904 | tf_op jit(solution)/shard_map/ppermute | solution.py:435
  48.6 3.6 %pairs.1 = (f32[256,128]{1,0:T(8,128)S(1)}, f32[256,128]{1,0:T(8,128)S(1)}) custom-call(f32[512,128]{1,0:T(8,128)S(1)} %bitcast.13, f32[256,128]{1,0:T(8,128)S(1)} %get-tuple-element.21.adj_ref, f32[128,128]{1,0:T(8,128)S(1)} %get-tuple-element.24.kernel_ref, s32[128,128]{1,0:T(8,128)S(1)} %get-tuple-element.25.target_ref), custom_call_target="tpu_custom_call" | custom-call | flops 4294967296 | bytes 8388608 | tf_op jit(solution)/shard_map/pairs/pallas_call | solution.py:440
  52.2 0.0 collective-permute-done.y_second_ref
  52.2 0.0 collective-permute-done.1.y_first_ref
  52.2 0.0 collective-permute-done.2.x_second_ref
  52.2 0.0 collective-permute-done.3.x_first_ref
  52.2 0.7 next.1
  53.0 25.3 %all_to_all.11 = f32[16,32,128]{2,1,0:T(8,128)S(1)} all-to-all(f32[16,32,128]{2,1,0:T(8,128)S(1)} %bitcast.16), channel_id=1, replica_groups=mesh['sec'=16,'gx'=16,'gy'=2] {'sec'}, dimensions={0} | all-to-all | bytes 524288 | tf_op jit(solution)/shard_map/all_to_all | solution.py:376
  78.2 1.0 %unpack.1 = (f32[256,128]{1,0:T(8,128)}, f32[256,128]{1,0:T(8,128)}) custom-call(f32[512,128]{1,0:T(8,128)S(1)} %bitcast.15), custom_call_target="tpu_custom_call" | custom-call | bytes 1048576 | tf_op jit(solution)/shard_map/unpack/pallas_call | solution.py:459
Async XLA Ops:
  35.6 16.6 %collective-permute-start = (f32[136,128]{1,0:T(8,128)S(1)}, f32[136,128]{1,0:T(8,128)S(1)}, u32[]{:S(2)}, u32[]{:S(2)}) collective-permute-start(f32[136,128]{1,0:T(8,128)S(1)} %get-tuple-element.28), channel_id=1, source_target_pairs={{32,64},{96,128},{160,192},{224,256},{288,320},{352,384},{416,448}... | collective-permute-start | bytes 208904 | tf_op jit(solution)/shard_map/ppermute | solution.py:438
  39.2 13.0 %collective-permute-start.1 = (f32[136,128]{1,0:T(8,128)S(1)}, f32[136,128]{1,0:T(8,128)S(1)}, u32[]{:S(2)}, u32[]{:S(2)}) collective-permute-start(f32[136,128]{1,0:T(8,128)S(1)} %get-tuple-element.29), channel_id=1, source_target_pairs={{0,32},{64,96},{128,160},{192,224},{256,288},{320,352},{384,416},{... | collective-permute-start | bytes 208904 | tf_op jit(solution)/shard_map/ppermute | solution.py:437
  43.2 9.0 %collective-permute-start.2 = (f32[136,128]{1,0:T(8,128)S(1)}, f32[136,128]{1,0:T(8,128)S(1)}, u32[]{:S(2)}, u32[]{:S(2)}) collective-permute-start(f32[136,128]{1,0:T(8,128)S(1)} %get-tuple-element.30), channel_id=1, source_target_pairs={{2,4},{6,8},{10,12},{14,16},{18,20},{22,24},{26,28},{30,0},{4,2},{... | collective-permute-start | bytes 208904 | tf_op jit(solution)/shard_map/ppermute | solution.py:436
  45.1 7.1 %collective-permute-start.3 = (f32[136,128]{1,0:T(8,128)S(1)}, f32[136,128]{1,0:T(8,128)S(1)}, u32[]{:S(2)}, u32[]{:S(2)}) collective-permute-start(f32[136,128]{1,0:T(8,128)S(1)} %get-tuple-element.31), channel_id=1, source_target_pairs={{0,2},{4,6},{8,10},{12,14},{16,18},{20,22},{24,26},{28,30},{2,0},{... | collective-permute-start | bytes 208904 | tf_op jit(solution)/shard_map/ppermute | solution.py:435
